TPU v7x, 256 devices: a whole 4x4x8 slice. The times are simulated.
256 devices in a mesh: tm: 4 (over x_lo, core), sx: 8 (over z), sy: 8 (over x_hi, y).
Axes of the slice: x: 4 (x_hi: 2, x_lo: 2; x = x_hi * 2 + x_lo), y: 4, z: 8, core: 2. Of those that a mesh axis runs over, the one named last changes fastest.
Arguments:
- right_side: float32 [4, 16, 64, 128, 128], P('tm', None, 'sx', 'sy'), may hold values from -6 to 6
- current: float32 [4, 16, 64, 128, 128], P('tm', None, 'sx', 'sy'), may hold values from -6 to 6
- classes: int32 [4, 64, 128, 128], P('tm', 'sx', 'sy'), may hold values from 0 to 7
- volume: float32 [8, 16, 16], replicated, may hold values from -0.35 to 12
- face_gain: float32 [8, 6], replicated, may hold values from 0.5 to 2
- time_gain: float32 [8], replicated, may hold values from 0.5 to 2
Outputs:
- smoothed: float32 [4, 16, 64, 128, 128], P('tm', None, 'sx', 'sy')
All inputs are finite; a program needn't handle non-finite values.
Results may differ from a plain program's by a relative error of at most 0.0001.
Values sent between devices are 32-bit elements; how exact they have to be, the bound alone decides.
No kernel may reach another device: no remote copies, remote signals or barrier semaphores. Data moves between devices by JAX's collectives and lax.ppermute only.
A program may use at most 64 MiB of HBM per device.

v0:
```python
import functools
import jax
import jax.numpy as jnp
from jax import lax
from jax.experimental import pallas as pl
from jax.experimental.pallas import tpu as pltpu
from jax.sharding import PartitionSpec as P

F32 = jnp.float32
BF16 = jnp.bfloat16
DAMP = 0.7
VMEM = pl.BlockSpec(memory_space=pltpu.VMEM)
SMEM = pl.BlockSpec(memory_space=pltpu.SMEM)
PARAMS = pltpu.CompilerParams(vmem_limit_bytes=40 * 1024 * 1024)


def bit_of(shape, dim, m):
    return (lax.broadcasted_iota(jnp.int32, shape, dim) & m) != 0


def split2(v):
    hi = v.astype(BF16)
    lo = (v - hi.astype(F32)).astype(BF16)
    return hi, lo


def pack_faces(lower, upper, m, want):
    keep = bit_of(lower.shape, 0, m) == want
    by = m if not want else 8 - m
    return jnp.where(keep, lower, pltpu.roll(upper, by, 0))


def unpack_faces(msg, m, want):
    by = 8 - m if not want else m
    return msg, pltpu.roll(msg, by, 0)


def emit(nx, ny, v_ref, xp_ref, xm_ref, yp_ref, ym_ref):
    def one(x, y, m, want):
        return pack_faces(v_ref[x, y, 0:8], v_ref[x, y, 8:16], m, want)

    for y in range(ny):
        xp_ref[y] = one(0, y, 4, False)
        xm_ref[y] = one(nx - 1, y, 4, True)
    for x in range(nx):
        yp_ref[x] = one(x, 0, 2, False)
        ym_ref[x] = one(x, ny - 1, 2, True)


def prep_kernel(nx, ny, u_ref, v_ref, up_ref, *faces):
    def plane(x, _):
        for y in range(ny):
            rows = u_ref[pl.ds(x * ny + y, 16, stride=nx * ny), :]
            v_ref[x, y] = rows
            up_ref[x, y] = rows[8:]
        return 0

    lax.fori_loop(0, nx, plane, 0)
    emit(nx, ny, v_ref, *faces)


def pack_kernel(nx, ny, v_ref, uh_ref, ul_ref, zh_ref, zl_ref):
    def plane(x, _):
        odd = bit_of((16, 128), 0, 1)
        for y in range(ny):
            u = v_ref[x, y]
            uh_ref[x, y], ul_ref[x, y] = split2(u)
            mixed = jnp.where(odd, pltpu.roll(u, 1, 1), pltpu.roll(u, 127, 1))
            zh_ref[x, y], zl_ref[x, y] = split2(mixed)
        return 0

    lax.fori_loop(0, nx, plane, 0)


def table_kernel(nx, ny, vol_ref, face_ref, time_ref, slab_ref, r_ref, w_ref, rh_ref, rl_ref):
    classes = face_ref.shape[0]
    lane = lax.broadcasted_iota(jnp.int32, (16, 128), 1)
    row = lax.broadcasted_iota(jnp.int32, (16, 128), 0)
    eye = jnp.where(lane == row + 16, 1.0, 0.0)
    mats = [vol_ref[c] + eye for c in range(classes)]
    for k in range(16):
        for c in range(classes):
            a = mats[c]
            column = jnp.broadcast_to(a[:, k : k + 1], (16, 128))
            pivot = jnp.broadcast_to(column[k : k + 1], (16, 128))
            scaled = jnp.broadcast_to(a[k : k + 1], (16, 128)) / pivot
            factor = jnp.where(row == k, column - 1.0, column)
            mats[c] = a - factor * scaled
    alive = jnp.where(slab_ref[0] > 0, 1.0, 0.0)
    for c in range(classes):
        base = jnp.where(lane < 16, pltpu.roll(mats[c], 112, 1), 0.0) * DAMP
        total = base
        for place, m, minus, plus in ((16, 4, 0, 1), (32, 2, 2, 3), (48, 1, 4, 5)):
            high = (lane & m) != 0
            swapped = jnp.where(high, pltpu.roll(base, m, 1), pltpu.roll(base, 128 - m, 1))
            gain = jnp.where(high, face_ref[c, minus], face_ref[c, plus])
            block = jnp.where(lane < 16, swapped * gain, 0.0)
            total = total + pltpu.roll(block, place, 1)
        timed = jnp.where(lane < 8, base * (time_ref[c] * alive), 0.0)
        hi, lo = split2(total)
        thi, tlo = split2(timed)
        hi, lo, thi, tlo = (v.astype(F32) for v in (hi, lo, thi, tlo))
        rows = pl.ds(c * 16, 16)
        w_ref[rows, 0:128] = (hi + pltpu.roll(hi, 64, 1)).astype(BF16)
        second = lo + pltpu.roll(thi, 64, 1) + pltpu.roll(thi, 72, 1)
        second = second + pltpu.roll(tlo, 80, 1) + pltpu.roll(tlo, 88, 1)
        w_ref[rows, 128:256] = second.astype(BF16)

    def plane(x, _):
        for y in range(ny):
            r = r_ref[pl.ds(x * ny + y, 16, stride=nx * ny), :]
            rh_ref[x, y], rl_ref[x, y] = split2(r)
        return 0

    lax.fori_loop(0, nx, plane, 0)


def sweep_kernel(nx, ny, last, *refs):
    (w_ref, cls_ref, v_ref, rh_ref, rl_ref, uh_ref, ul_ref, zh_ref, zl_ref,
     before_ref, hxp_ref, hxm_ref, hyp_ref, hym_ref, *outs) = refs
    if last:
        out_ref, xph, xpl, xmh, xml, yph, ypl, ymh, yml = outs
    else:
        n_ref, up_ref, xp_ref, xm_ref, yp_ref, ym_ref, xph, xpl, xmh, xml, yph, ypl, ymh, yml = outs
    for src, hi_ref, lo_ref, m, want, count in (
        (hxp_ref, xph, xpl, 4, False, ny),
        (hxm_ref, xmh, xml, 4, True, ny),
        (hyp_ref, yph, ypl, 2, False, nx),
        (hym_ref, ymh, yml, 2, True, nx),
    ):
        for i in range(count):
            whole = jnp.concatenate(unpack_faces(src[i], m, want), axis=0)
            hi_ref[i], lo_ref[i] = split2(whole)
    xbit = bit_of((16, 128), 0, 4)
    ybit = bit_of((16, 128), 0, 2)

    def stack(x, y):
        tiles = []
        for uref, rref, zref, xp, xm, yp, ym in (
            (uh_ref, rh_ref, zh_ref, xph, xmh, yph, ymh),
            (ul_ref, rl_ref, zl_ref, xpl, xml, ypl, yml),
        ):
            ahead = jnp.where(x == nx - 1, xp[y], uref[jnp.minimum(x + 1, nx - 1), y])
            behind = jnp.where(x == 0, xm[y], uref[jnp.maximum(x - 1, 0), y])
            along_x = jnp.where(xbit, behind, ahead)
            right = yp[x] if y == ny - 1 else uref[x, y + 1]
            left = ym[x] if y == 0 else uref[x, y - 1]
            along_y = jnp.where(ybit, left, right)
            tiles.append([rref[x, y], along_x, along_y, zref[x, y]])
        b = before_ref[x, y]
        bh = b.astype(BF16).astype(F32)
        timed = jnp.concatenate([bh, b - bh], axis=0).astype(BF16)
        return jnp.concatenate(tiles[0] + tiles[1] + tiles[0] + [timed, timed], axis=0)

    def plane(x, _):
        for y in range(0, ny, 2):
            s = jnp.concatenate([stack(x, y), stack(x, y + 1)], axis=1)
            product = jnp.dot(w_ref[:, 0:224], s, preferred_element_type=F32)
            for k in range(2):
                cls = jnp.broadcast_to(cls_ref[x, y + k : y + k + 1, :], (8, 128))
                masks = [(cls & m) != 0 for m in (1, 2, 4)]
                halves = []
                for h in range(2):
                    level = [
                        product[c * 16 + h * 8 : c * 16 + h * 8 + 8, k * 128 : k * 128 + 128]
                        for c in range(8)
                    ]
                    for mask in masks:
                        level = [
                            jnp.where(mask, level[i + 1], level[i]) for i in range(0, len(level), 2)
                        ]
                    halves.append((1.0 - DAMP) * v_ref[x, y + k, h * 8 : h * 8 + 8] + level[0])
                whole = jnp.concatenate(halves, axis=0)
                if last:
                    out_ref[pl.ds(x * ny + y + k, 16, stride=nx * ny), :] = whole
                else:
                    n_ref[x, y + k] = whole
                    up_ref[x, y + k] = halves[1]
        return 0

    lax.fori_loop(0, nx, plane, 0)
    if not last:
        emit(nx, ny, n_ref, xp_ref, xm_ref, yp_ref, ym_ref)


def ring(axis, by):
    n = lax.axis_size(axis)
    return [(i, (i + by) % n) for i in range(n)]


def exchange(up, xp, xm, yp, ym):
    before = lax.ppermute(up, "tm", ring("tm", 1))
    hxp = lax.ppermute(xp, "sx", ring("sx", -1))
    hxm = lax.ppermute(xm, "sx", ring("sx", 1))
    hyp = lax.ppermute(yp, "sy", ring("sy", -1))
    hym = lax.ppermute(ym, "sy", ring("sy", 1))
    return before, hxp, hxm, hyp, hym


def call(kernel, ins, outs, name, scratch=(), flops=10**9, params=PARAMS):
    return pl.pallas_call(
        kernel,
        in_specs=ins,
        out_specs=[VMEM] * len(outs),
        out_shape=outs,
        scratch_shapes=scratch,
        compiler_params=params,
        cost_estimate=pl.CostEstimate(flops=flops, bytes_accessed=4 * 10**6, transcendentals=0),
        name=name,
    )


def on_device(right_side, current, classes, volume, face_gain, time_gain):
    _, nodes, nx, ny, nz = current.shape
    shape = jax.ShapeDtypeStruct
    faces = [shape((n, 8, nz), F32) for n in (ny, ny, nx, nx)]
    field = shape((nx, ny, nodes, nz), F32)
    half = shape((nx, ny, 8, nz), F32)
    packed = shape((nx, ny, nodes, nz), BF16)
    flat = (nodes * nx * ny, nz)
    u = current.reshape(flat)
    r = right_side.reshape(flat)
    cls = classes[0]
    slab = lax.axis_index("tm").reshape(1)
    vol = jnp.pad(volume, ((0, 0), (0, 0), (0, 112)))

    v, *sent = call(
        functools.partial(prep_kernel, nx, ny), [VMEM], [field, half] + faces, "prep"
    )(u)
    got = exchange(*sent)
    w, rh, rl = call(
        functools.partial(table_kernel, nx, ny),
        [VMEM, SMEM, SMEM, SMEM, VMEM],
        [shape((8 * nodes, 256), BF16), packed, packed],
        "tables",
    )(vol, face_gain, time_gain, slab, r)
    pack = call(functools.partial(pack_kernel, nx, ny), [VMEM], [packed] * 4, "pack")
    scratch = [pltpu.VMEM((n, 16, nz), BF16) for n in (ny, ny, ny, ny, nx, nx, nx, nx)]
    views = pack(v)
    v, *sent = call(
        functools.partial(sweep_kernel, nx, ny, False),
        [VMEM] * 14, [field, half] + faces, "sweep_a", scratch,
    )(w, cls, v, rh, rl, *views, *got)
    got = exchange(*sent)
    views = pack(v)
    (out,) = call(
        functools.partial(sweep_kernel, nx, ny, True),
        [VMEM] * 14, [shape(flat, F32)], "sweep_b", scratch,
    )(w, cls, v, rh, rl, *views, *got)
    return out.reshape(current.shape)


def solution(mesh):
    placed = (
        P("tm", None, "sx", "sy", None),
        P("tm", None, "sx", "sy", None),
        P("tm", "sx", "sy", None),
        P(),
        P(),
        P(),
    )
    return jax.shard_map(
        on_device,
        mesh=mesh,
        in_specs=placed,
        out_specs=P("tm", None, "sx", "sy", None),
        check_vma=False,
    )
```

profile of v0, /device:TPU:1, one launch (start us, length us, event | category | flops | bytes accessed | tf_op | source)
XLA Modules:
  0.0 40.9 jit_solution(8724493446812181562)
XLA Ops:
  0.0 1.2 %copy-done.1 = f32[1,16,8,16,128]{4,3,2,1,0:T(8,128)S(1)} copy-done((f32[1,16,8,16,128]{4,3,2,1,0:T(8,128)S(1)}, f32[1,16,8,16,128]{4,3,2,1,0:T(8,128)}, u32[]{:S(2)}) %copy-start.1) | copy-done | bytes 1048600
  1.2 0.7 %prep.1 = (f32[8,16,16,128]{3,2,1,0:T(8,128)S(1)}, f32[8,16,8,128]{3,2,1,0:T(8,128)S(1)}, f32[16,8,128]{2,1,0:T(8,128)S(1)}, f32[16,8,128]{2,1,0:T(8,128)S(1)}, ...) custom-call(f32[2048,128]{1,0:T(8,128)S(1)} %bitcast.7), custom_call_target="tpu_custom_call" | custom-call | flops 1000000000 | bytes 4000000 | tf_op jit(solution)/shard_map/prep/pallas_call | solution.py:227
  1.9 2.7 %collective-permute-start = (f32[8,16,8,128]{3,2,1,0:T(8,128)S(1)}, f32[8,16,8,128]{3,2,1,0:T(8,128)S(1)}, u32[]{:S(2)}, u32[]{:S(2)}) collective-permute-start(f32[8,16,8,128]{3,2,1,0:T(8,128)S(1)} %get-tuple-element.36), channel_id=1, source_target_pairs={{0,64},{64,128},{128,192},{192,0},{1,65},{65,129},{129,193},{193,1... | collective-permute-start | bytes 1572872 | tf_op jit(solution)/shard_map/ppermute | solution.py:192
  4.6 4.9 %collective-permute-start.3 = (f32[8,8,128]{2,1,0:T(8,128)S(1)}, f32[8,8,128]{2,1,0:T(8,128)S(1)}, u32[]{:S(2)}, u32[]{:S(2)}) collective-permute-start(f32[8,8,128]{2,1,0:T(8,128)S(1)} %get-tuple-element.39), channel_id=1, source_target_pairs={{0,7},{1,0},{2,1},{3,2},{4,3},{5,4},{6,5},{7,6},{8,15},{9,8},{10,9... | collective-permute-start | bytes 98312 | tf_op jit(solution)/shard_map/ppermute | solution.py:195
  9.5 0.0 collective-permute-start.4
  9.5 5.6 %collective-permute-start.1 = (f32[16,8,128]{2,1,0:T(8,128)S(1)}, f32[16,8,128]{2,1,0:T(8,128)S(1)}, u32[]{:S(2)}, u32[]{:S(2)}) collective-permute-start(f32[16,8,128]{2,1,0:T(8,128)S(1)} %get-tuple-element.37), channel_id=1, source_target_pairs={{0,56},{8,0},{16,8},{24,16},{32,24},{40,32},{48,40},{56,48},{1,57}... | collective-permute-start | bytes 196616 | tf_op jit(solution)/shard_map/ppermute | solution.py:193
  15.1 0.0 collective-permute-start.2
  15.1 0.0 copy-start.2
  15.1 0.0 copy-start.3
  15.1 1.1 %pack.2 = (bf16[8,16,16,128]{3,2,1,0:T(8,128)(2,1)S(1)}, bf16[8,16,16,128]{3,2,1,0:T(8,128)(2,1)S(1)}, bf16[8,16,16,128]{3,2,1,0:T(8,128)(2,1)S(1)}, bf16[8,16,16,128]{3,2,1,0:T(8,128)(2,1)S(1)}) custom-call(f32[8,16,16,128]{3,2,1,0:T(8,128)S(1)} %get-tuple-element.29.v_ref.refs_2_), custom_call_target="tpu_custom_call" | custom-call | flops 1000000000 | bytes 4000000 | tf_op jit(solution)/shard_map/pack/pallas_call | solution.py:239
  16.2 0.0 copy-start.4
  16.2 0.1 copy-done.2
  16.3 0.6 %copy-done.4 = f32[8]{0:T(128)S(1)} copy-done((f32[8]{0:T(128)S(1)}, f32[8]{0:T(128)}, u32[]{:S(2)}) %copy-start.4) | copy-done | bytes 56
  16.9 3.6 %tables.1 = (bf16[128,256]{1,0:T(8,128)(2,1)S(1)}, bf16[8,16,16,128]{3,2,1,0:T(8,128)(2,1)S(1)}, bf16[8,16,16,128]{3,2,1,0:T(8,128)(2,1)S(1)}) custom-call(f32[8,16,128]{2,1,0:T(8,128)S(1)} %pad.4.vol_ref, f32[8,6]{1,0:T(8,128)S(1)} %copy-done.3, f32[8]{0:T(128)S(1)} %copy-done.4, s32[1]{0:T(128)} %bitcast.slab_ref, f32[2048,128]{1,0:T(8,128)S(1)} %bitcast.8), custom_call_target="tpu_custom_call" | custom-call | flops 1000000000 | bytes 4000000 | tf_op jit(solution)/shard_map/tables/pallas_call | solution.py:231
  20.5 0.0 collective-permute-done.3.refs_12_
  20.5 0.0 collective-permute-done.4.refs_13_
  20.5 0.0 collective-permute-done.1.refs_10_
  20.5 0.0 collective-permute-done.2.refs_11_
  20.5 0.0 collective-permute-done.refs_9_
  20.6 2.6 %sweep_a.1 = (f32[8,16,16,128]{3,2,1,0:T(8,128)S(1)}, f32[8,16,8,128]{3,2,1,0:T(8,128)S(1)}, f32[16,8,128]{2,1,0:T(8,128)S(1)}, f32[16,8,128]{2,1,0:T(8,128)S(1)...) custom-call(bf16[128,256]{1,0:T(8,128)(2,1)S(1)} %get-tuple-element.28.refs_0_, s32[8,16,128]{2,1,0:T(8,128)S(1)} %bitcast.5, ...), custom_call_target="tpu_custom_call" | custom-call | flops 1000000000 | bytes 4000000 | tf_op jit(solution)/shard_map/sweep_a/pallas_call | solution.py:240
  23.2 0.1 collective-permute-start.5
  23.3 6.0 %collective-permute-start.8 = (f32[8,8,128]{2,1,0:T(8,128)S(1)}, f32[8,8,128]{2,1,0:T(8,128)S(1)}, u32[]{:S(2)}, u32[]{:S(2)}) collective-permute-start(f32[8,8,128]{2,1,0:T(8,128)S(1)} %get-tuple-element.49), channel_id=1, source_target_pairs={{0,7},{1,0},{2,1},{3,2},{4,3},{5,4},{6,5},{7,6},{8,15},{9,8},{10,9... | collective-permute-start | bytes 98312 | tf_op jit(solution)/shard_map/ppermute | solution.py:195
  29.3 0.0 collective-permute-start.9
  29.3 3.0 %collective-permute-start.6 = (f32[16,8,128]{2,1,0:T(8,128)S(1)}, f32[16,8,128]{2,1,0:T(8,128)S(1)}, u32[]{:S(2)}, u32[]{:S(2)}) collective-permute-start(f32[16,8,128]{2,1,0:T(8,128)S(1)} %get-tuple-element.47), channel_id=1, source_target_pairs={{0,56},{8,0},{16,8},{24,16},{32,24},{40,32},{48,40},{56,48},{1,57}... | collective-permute-start | bytes 196616 | tf_op jit(solution)/shard_map/ppermute | solution.py:193
  32.2 0.0 collective-permute-start.7
  32.3 1.1 %pack.3 = (bf16[8,16,16,128]{3,2,1,0:T(8,128)(2,1)S(1)}, bf16[8,16,16,128]{3,2,1,0:T(8,128)(2,1)S(1)}, bf16[8,16,16,128]{3,2,1,0:T(8,128)(2,1)S(1)}, bf16[8,16,16,128]{3,2,1,0:T(8,128)(2,1)S(1)}) custom-call(f32[8,16,16,128]{3,2,1,0:T(8,128)S(1)} %get-tuple-element.41.v_ref.refs_2_), custom_call_target="tpu_custom_call" | custom-call | flops 1000000000 | bytes 4000000 | tf_op jit(solution)/shard_map/pack/pallas_call | solution.py:245
  33.4 0.0 collective-permute-done.8.refs_12_
  33.4 3.3 %collective-permute-done.9.refs_13_ = f32[8,8,128]{2,1,0:T(8,128)S(1)} collective-permute-done((f32[8,8,128]{2,1,0:T(8,128)S(1)}, f32[8,8,128]{2,1,0:T(8,128)S(1)}, u32[]{:S(2)}, u32[]{:S(2)}) %collective-permute-start.9) | collective-permute-done | bytes 32800 | tf_op jit(solution)/shard_map/ppermute | solution.py:196
  36.7 0.0 collective-permute-done.6.refs_10_
  36.7 0.5 %collective-permute-done.7.refs_11_ = f32[16,8,128]{2,1,0:T(8,128)S(1)} collective-permute-done((f32[16,8,128]{2,1,0:T(8,128)S(1)}, f32[16,8,128]{2,1,0:T(8,128)S(1)}, u32[]{:S(2)}, u32[]{:S(2)}) %collective-permute-start.7) | collective-permute-done | bytes 65568 | tf_op jit(solution)/shard_map/ppermute | solution.py:194
  37.2 0.0 collective-permute-done.5.refs_9_
  37.2 3.6 %sweep_b.1 = f32[2048,128]{1,0:T(8,128)} custom-call(bf16[128,256]{1,0:T(8,128)(2,1)S(1)} %get-tuple-element.28.refs_0_, s32[8,16,128]{2,1,0:T(8,128)S(1)} %bitcast.6, f32[8,16,16,128]{3,2,1,0:T(8,128)S(1)} %get-tuple-element.41.v_ref.refs_2_, bf16[8,16,16,128]{3,2,1,0:T(8,128)(2,1)S(1)} %get-tuple-element.30.refs_3_, ...), custom_call_target="tpu_custom_call" | custom-call | flops 1000000000 | bytes 4000000 | tf_op jit(solution)/shard_map/sweep_b/pallas_call | solution.py:246
  (7 shorter events, 0.0 us)
Async XLA Ops:
  0.0 1.2 %copy-start.1 = (f32[1,16,8,16,128]{4,3,2,1,0:T(8,128)S(1)}, f32[1,16,8,16,128]{4,3,2,1,0:T(8,128)}, u32[]{:S(2)}) copy-start(f32[1,16,8,16,128]{4,3,2,1,0:T(8,128)} %param.7) | copy-start | bytes 3145732
  1.2 13.8 %copy-start.5 = (f32[8,16,16]{2,1,0:T(8,128)S(1)}, f32[8,16,16]{2,1,0:T(8,128)}, u32[]{:S(2)}) copy-start(f32[8,16,16]{2,1,0:T(8,128)} %param.9) | copy-start | bytes 24580
  1.9 18.6 %collective-permute-start = (f32[8,16,8,128]{3,2,1,0:T(8,128)S(1)}, f32[8,16,8,128]{3,2,1,0:T(8,128)S(1)}, u32[]{:S(2)}, u32[]{:S(2)}) collective-permute-start(f32[8,16,8,128]{3,2,1,0:T(8,128)S(1)} %get-tuple-element.36), channel_id=1, source_target_pairs={{0,64},{64,128},{128,192},{192,0},{1,65},{65,129},{129,193},{193,1... | collective-permute-start | bytes 1572872 | tf_op jit(solution)/shard_map/ppermute | solution.py:192
  4.6 15.9 %collective-permute-start.3 = (f32[8,8,128]{2,1,0:T(8,128)S(1)}, f32[8,8,128]{2,1,0:T(8,128)S(1)}, u32[]{:S(2)}, u32[]{:S(2)}) collective-permute-start(f32[8,8,128]{2,1,0:T(8,128)S(1)} %get-tuple-element.39), channel_id=1, source_target_pairs={{0,7},{1,0},{2,1},{3,2},{4,3},{5,4},{6,5},{7,6},{8,15},{9,8},{10,9... | collective-permute-start | bytes 98312 | tf_op jit(solution)/shard_map/ppermute | solution.py:195
  9.5 11.0 %collective-permute-start.4 = (f32[8,8,128]{2,1,0:T(8,128)S(1)}, f32[8,8,128]{2,1,0:T(8,128)S(1)}, u32[]{:S(2)}, u32[]{:S(2)}) collective-permute-start(f32[8,8,128]{2,1,0:T(8,128)S(1)} %get-tuple-element.40), channel_id=1, source_target_pairs={{0,1},{1,2},{2,3},{3,4},{4,5},{5,6},{6,7},{7,0},{8,9},{9,10},{10,1... | collective-permute-start | bytes 98312 | tf_op jit(solution)/shard_map/ppermute | solution.py:196
  9.5 11.0 %collective-permute-start.1 = (f32[16,8,128]{2,1,0:T(8,128)S(1)}, f32[16,8,128]{2,1,0:T(8,128)S(1)}, u32[]{:S(2)}, u32[]{:S(2)}) collective-permute-start(f32[16,8,128]{2,1,0:T(8,128)S(1)} %get-tuple-element.37), channel_id=1, source_target_pairs={{0,56},{8,0},{16,8},{24,16},{32,24},{40,32},{48,40},{56,48},{1,57}... | collective-permute-start | bytes 196616 | tf_op jit(solution)/shard_map/ppermute | solution.py:193
  15.1 5.5 %collective-permute-start.2 = (f32[16,8,128]{2,1,0:T(8,128)S(1)}, f32[16,8,128]{2,1,0:T(8,128)S(1)}, u32[]{:S(2)}, u32[]{:S(2)}) collective-permute-start(f32[16,8,128]{2,1,0:T(8,128)S(1)} %get-tuple-element.38), channel_id=1, source_target_pairs={{0,8},{8,16},{16,24},{24,32},{32,40},{40,48},{48,56},{56,0},{1,9},... | collective-permute-start | bytes 196616 | tf_op jit(solution)/shard_map/ppermute | solution.py:194
  15.1 1.2 %copy-start.2 = (f32[1,16,8,16,128]{4,3,2,1,0:T(8,128)S(1)}, f32[1,16,8,16,128]{4,3,2,1,0:T(8,128)}, u32[]{:S(2)}) copy-start(f32[1,16,8,16,128]{4,3,2,1,0:T(8,128)} %param.6) | copy-start | bytes 3145732
  15.1 1.2 %copy-start.3 = (f32[8,6]{1,0:T(8,128)S(1)}, f32[8,6]{1,0:T(8,128)}, u32[]{:S(2)}) copy-start(f32[8,6]{1,0:T(8,128)} %face_ref.1) | copy-start | bytes 580
  16.2 0.7 %copy-start.4 = (f32[8]{0:T(128)S(1)}, f32[8]{0:T(128)}, u32[]{:S(2)}) copy-start(f32[8]{0:T(128)} %time_ref.1) | copy-start | bytes 100
  16.9 3.7 %copy-start = (s32[1,8,16,128]{3,2,1,0:T(8,128)S(1)}, s32[1,8,16,128]{3,2,1,0:T(8,128)}, u32[]{:S(2)}) copy-start(s32[1,8,16,128]{3,2,1,0:T(8,128)} %param.8) | copy-start | bytes 196612
  23.2 14.0 %collective-permute-start.5 = (f32[8,16,8,128]{3,2,1,0:T(8,128)S(1)}, f32[8,16,8,128]{3,2,1,0:T(8,128)S(1)}, u32[]{:S(2)}, u32[]{:S(2)}) collective-permute-start(f32[8,16,8,128]{3,2,1,0:T(8,128)S(1)} %get-tuple-element.46), channel_id=1, source_target_pairs={{0,64},{64,128},{128,192},{192,0},{1,65},{65,129},{129,193},{193,1... | collective-permute-start | bytes 1572872 | tf_op jit(solution)/shard_map/ppermute | solution.py:192
  23.3 10.0 %collective-permute-start.8 = (f32[8,8,128]{2,1,0:T(8,128)S(1)}, f32[8,8,128]{2,1,0:T(8,128)S(1)}, u32[]{:S(2)}, u32[]{:S(2)}) collective-permute-start(f32[8,8,128]{2,1,0:T(8,128)S(1)} %get-tuple-element.49), channel_id=1, source_target_pairs={{0,7},{1,0},{2,1},{3,2},{4,3},{5,4},{6,5},{7,6},{8,15},{9,8},{10,9... | collective-permute-start | bytes 98312 | tf_op jit(solution)/shard_map/ppermute | solution.py:195
  29.3 7.4 %collective-permute-start.9 = (f32[8,8,128]{2,1,0:T(8,128)S(1)}, f32[8,8,128]{2,1,0:T(8,128)S(1)}, u32[]{:S(2)}, u32[]{:S(2)}) collective-permute-start(f32[8,8,128]{2,1,0:T(8,128)S(1)} %get-tuple-element.50), channel_id=1, source_target_pairs={{0,1},{1,2},{2,3},{3,4},{4,5},{5,6},{6,7},{7,0},{8,9},{9,10},{10,1... | collective-permute-start | bytes 98312 | tf_op jit(solution)/shard_map/ppermute | solution.py:196
  29.3 7.4 %collective-permute-start.6 = (f32[16,8,128]{2,1,0:T(8,128)S(1)}, f32[16,8,128]{2,1,0:T(8,128)S(1)}, u32[]{:S(2)}, u32[]{:S(2)}) collective-permute-start(f32[16,8,128]{2,1,0:T(8,128)S(1)} %get-tuple-element.47), channel_id=1, source_target_pairs={{0,56},{8,0},{16,8},{24,16},{32,24},{40,32},{48,40},{56,48},{1,57}... | collective-permute-start | bytes 196616 | tf_op jit(solution)/shard_map/ppermute | solution.py:193
  32.2 5.0 %collective-permute-start.7 = (f32[16,8,128]{2,1,0:T(8,128)S(1)}, f32[16,8,128]{2,1,0:T(8,128)S(1)}, u32[]{:S(2)}, u32[]{:S(2)}) collective-permute-start(f32[16,8,128]{2,1,0:T(8,128)S(1)} %get-tuple-element.48), channel_id=1, source_target_pairs={{0,8},{8,16},{16,24},{24,32},{32,40},{40,48},{48,56},{56,0},{1,9},... | collective-permute-start | bytes 196616 | tf_op jit(solution)/shard_map/ppermute | solution.py:194
where the time goes:
time: 41 us; the launch traced here: 40.9 us
  starting transfers between devices  22.2 us (54%)
  Pallas kernels  12.7 us (31%)
  waiting for transfers between devices  3.89 us (9%)
  local copies, waits for them, and re-layouts  1.92 us (5%)
    ppermute x2, starting transfers between devices, exchange(): hyp = lax.ppermute(yp, 'sy', ring('sy', -1))  10.9 us
    ppermute x2, starting transfers between devices, exchange(): hxp = lax.ppermute(xp, 'sx', ring('sx', -1))  8.53 us
    pallas_call x1, Pallas kernels, on_device(): call(functools.partial(sweep_kernel, nx, ny, True), [VMEM] * 14, [shape(f...  3.64 us
    pallas_call x1, Pallas kernels, on_device(): call(functools.partial(table_kernel, nx, ny), [VMEM, SMEM, SMEM, SMEM, VM...  3.59 us
    ppermute x2, waiting for transfers between devices, exchange(): hym = lax.ppermute(ym, 'sy', ring('sy', 1))  3.34 us
    ppermute x2, starting transfers between devices, exchange(): before = lax.ppermute(up, 'tm', ring('tm', 1))  2.8 us
    pallas_call x1, Pallas kernels, on_device(): call(functools.partial(sweep_kernel, nx, ny, False), [VMEM] * 14, [field,...  2.64 us
    pallas_call x2, Pallas kernels, on_device(): views = pack(v)  2.2 us
  transfers between devices with their start and end apart: 10, of which 2 were waited for; matrix products, arithmetic and copies ran while one was open for 0% of the time, Pallas kernels for 14%

commit v1 on v0

v1 whole, which is shorter than its diff:
```python
import functools
import jax
import jax.numpy as jnp
from jax import lax
from jax.experimental import pallas as pl
from jax.experimental.pallas import tpu as pltpu
from jax.sharding import PartitionSpec as P

F32 = jnp.float32
BF16 = jnp.bfloat16
DAMP = 0.7
GROUP = 4
VMEM = pl.BlockSpec(memory_space=pltpu.VMEM)
HBM = pl.BlockSpec(memory_space=pltpu.HBM)


def bit_of(shape, dim, m):
    return (lax.broadcasted_iota(jnp.int32, shape, dim) & m) != 0


def split2(v):
    hi = v.astype(BF16)
    lo = (v - hi.astype(F32)).astype(BF16)
    return hi, lo


def pack_faces(lower, upper, m, want):
    keep = bit_of(lower.shape, 0, m) == want
    by = m if not want else 8 - m
    return jnp.where(keep, lower, pltpu.roll(upper, by, 0))


def unpack_faces(msg, m, want):
    by = 8 - m if not want else m
    return msg, pltpu.roll(msg, by, 0)


def emit(nx, ny, place_ref, v_ref, xa_ref, xb_ref, ya_ref, yb_ref):
    def one(x, y, m, want):
        return pack_faces(v_ref[x, y, 0:8], v_ref[x, y, 8:16], m, want)

    def put(a_ref, b_ref, i, even, near, far):
        a_ref[i] = jnp.where(even, far, near)
        b_ref[i] = jnp.where(even, near, far)

    even_x = place_ref[1] == 0
    even_y = place_ref[2] == 0
    for y in range(ny):
        put(xa_ref, xb_ref, y, even_x, one(0, y, 4, False), one(nx - 1, y, 4, True))
    for x in range(nx):
        put(ya_ref, yb_ref, x, even_y, one(x, 0, 2, False), one(x, ny - 1, 2, True))


def prep_kernel(nx, ny, place_ref, u_ref, v_ref, up_ref, *rest):
    *faces, held_ref, sems = rest

    def copy(x):
        rows = pl.ds(x * ny, ny)
        return pltpu.make_async_copy(u_ref.at[:, rows], held_ref.at[:, rows], sems.at[x])

    for x in range(nx):
        copy(x).start()
    flat_ref = held_ref.reshape(16 * nx * ny, 128)

    for x in range(nx):
        copy(x).wait()
        for y in range(ny):
            rows = flat_ref[pl.ds(x * ny + y, 16, stride=nx * ny), :]
            v_ref[x, y] = rows
            up_ref[x, y] = rows[8:]
    emit(nx, ny, place_ref, v_ref, *faces)


def pack_kernel(nx, ny, v_ref, uh_ref, ul_ref, zh_ref, zl_ref):
    odd = bit_of((16, 128), 0, 1)
    for x in range(nx):
        for y in range(ny):
            u = v_ref[x, y]
            uh_ref[x, y], ul_ref[x, y] = split2(u)
            mixed = jnp.where(odd, pltpu.roll(u, 1, 1), pltpu.roll(u, 127, 1))
            zh_ref[x, y], zl_ref[x, y] = split2(mixed)


def inverses(vol_ref, wide_ref):
    lane = lax.broadcasted_iota(jnp.int32, (16, 128), 1)
    row = lax.broadcasted_iota(jnp.int32, (16, 128), 0)
    wide_ref[...] = jnp.zeros((128, 128), F32)
    wide_ref[:, 0:16] = vol_ref[...]
    turned = jnp.transpose(wide_ref[...])[0:16]
    mats = [turned if i == 0 else pltpu.roll(turned, 128 - i, 1) for i in range(16)]
    for k in range(16):
        scaled = jnp.where(row == k, 1.0, mats[k]) * (1.0 / mats[k][k : k + 1])
        for i in range(16):
            if i != k:
                factor = jnp.broadcast_to(mats[i][k : k + 1], (16, 128))
                mats[i] = jnp.where(row == k, 0.0, mats[i]) - factor * scaled
        mats[k] = scaled
    held = [jnp.where(lane % 16 == 0, m, 0.0) for m in mats]
    total = held[0]
    for i in range(1, 16):
        total = total + pltpu.roll(held[i], i, 1)
    return jnp.transpose(jnp.concatenate([total, jnp.zeros((112, 128), F32)], axis=0))


def table_kernel(nx, ny, place_ref, vol_ref, face_ref, time_ref, r_ref, w_ref, rh_ref, rl_ref, wide_ref):
    classes = face_ref.shape[0]
    lane = lax.broadcasted_iota(jnp.int32, (16, 128), 1)
    inverse = inverses(vol_ref, wide_ref)
    alive = jnp.where(place_ref[0, 0:1] > 0, 1.0, 0.0)
    spread = [jnp.broadcast_to(face_ref[:, k : k + 1], (classes, 128)) for k in range(6)]
    for c in range(classes):
        base = inverse[c * 16 : c * 16 + 16] * DAMP
        total = base
        for place, m, minus, plus in ((16, 4, 0, 1), (32, 2, 2, 3), (48, 1, 4, 5)):
            high = (lane & m) != 0
            swapped = jnp.where(high, pltpu.roll(base, m, 1), pltpu.roll(base, 128 - m, 1))
            gain = jnp.where(high, spread[minus][c : c + 1], spread[plus][c : c + 1])
            block = jnp.where(lane < 16, swapped * gain, 0.0)
            total = total + pltpu.roll(block, place, 1)
        gain = jnp.broadcast_to(time_ref[:, c : c + 1], (1, 128)) * alive
        timed = jnp.where(lane < 8, base * gain, 0.0)
        hi, lo = split2(total)
        thi, tlo = split2(timed)
        hi, lo, thi, tlo = (v.astype(F32) for v in (hi, lo, thi, tlo))
        rows = pl.ds(c * 16, 16)
        w_ref[rows, 0:128] = (hi + pltpu.roll(hi, 64, 1)).astype(BF16)
        second = lo + pltpu.roll(thi, 64, 1) + pltpu.roll(thi, 72, 1)
        second = second + pltpu.roll(tlo, 80, 1) + pltpu.roll(tlo, 88, 1)
        w_ref[rows, 128:256] = second.astype(BF16)

    for x in range(nx):
        for y in range(ny):
            r = r_ref[pl.ds(x * ny + y, 16, stride=nx * ny), :]
            rh_ref[x, y], rl_ref[x, y] = split2(r)


def sweep_kernel(nx, ny, last, *refs):
    (place_ref, w_ref, cls_ref, v_ref, rh_ref, rl_ref, uh_ref, ul_ref, zh_ref, zl_ref,
     before_ref, hxa_ref, hxb_ref, hyb_ref, hya_ref, *outs) = refs
    if last:
        out_ref, held_ref, sems, row_ref, xph, xpl, xmh, xml, yph, ypl, ymh, yml = outs
    else:
        n_ref, up_ref, xa_ref, xb_ref, ya_ref, yb_ref, xph, xpl, xmh, xml, yph, ypl, ymh, yml = outs
    even_x = place_ref[1] == 0
    even_y = place_ref[2] == 0
    for even, one_ref, two_ref, hi_ref, lo_ref, m, want, count in (
        (even_x, hxa_ref, hxb_ref, xph, xpl, 4, False, ny),
        (even_x, hxb_ref, hxa_ref, xmh, xml, 4, True, ny),
        (even_y, hya_ref, hyb_ref, yph, ypl, 2, False, nx),
        (even_y, hyb_ref, hya_ref, ymh, yml, 2, True, nx),
    ):
        for i in range(count):
            msg = jnp.where(even, one_ref[i], two_ref[i])
            whole = jnp.concatenate(unpack_faces(msg, m, want), axis=0)
            hi_ref[i], lo_ref[i] = split2(whole)
    xbit = bit_of((16, 128), 0, 4)
    ybit = bit_of((16, 128), 0, 2)

    def stack(x, y):
        tiles = []
        for uref, rref, zref, xp, xm, yp, ym in (
            (uh_ref, rh_ref, zh_ref, xph, xmh, yph, ymh),
            (ul_ref, rl_ref, zl_ref, xpl, xml, ypl, yml),
        ):
            ahead = xp[y] if x == nx - 1 else uref[x + 1, y]
            behind = xm[y] if x == 0 else uref[x - 1, y]
            along_x = jnp.where(xbit, behind, ahead)
            right = yp[x] if y == ny - 1 else uref[x, y + 1]
            left = ym[x] if y == 0 else uref[x, y - 1]
            along_y = jnp.where(ybit, left, right)
            tiles.append([rref[x, y], along_x, along_y, zref[x, y]])
        b = before_ref[x, y]
        bh = b.astype(BF16).astype(F32)
        timed = jnp.concatenate([bh, b - bh], axis=0).astype(BF16)
        return jnp.concatenate(tiles[0] + tiles[1] + tiles[0] + [timed, timed], axis=0)

    def copy(x):
        rows = pl.ds(x * ny, ny)
        return pltpu.make_async_copy(held_ref.at[:, rows], out_ref.at[:, rows], sems.at[x])

    def turn(x):
        for node in range(16):
            for y in range(0, ny, 8):
                rows = row_ref[pl.ds((x * ny + y) * 16 + node, 8, stride=16), :]
                held_ref[node, x * ny + y : x * ny + y + 8, :] = rows

    def plane(x):
        for y in range(0, ny, 2):
            s = jnp.concatenate([stack(x, y), stack(x, y + 1)], axis=1)
            product = jnp.dot(w_ref[:, 0:224], s, preferred_element_type=F32)
            for k in range(2):
                cls = jnp.broadcast_to(cls_ref[x, y + k : y + k + 1, :], (8, 128))
                masks = [(cls & m) != 0 for m in (1, 2, 4)]
                halves = []
                for h in range(2):
                    level = [
                        product[c * 16 + h * 8 : c * 16 + h * 8 + 8, k * 128 : k * 128 + 128]
                        for c in range(8)
                    ]
                    for mask in masks:
                        level = [
                            jnp.where(mask, level[i + 1], level[i]) for i in range(0, len(level), 2)
                        ]
                    halves.append((1.0 - DAMP) * v_ref[x, y + k, h * 8 : h * 8 + 8] + level[0])
                whole = jnp.concatenate(halves, axis=0)
                if last:
                    row_ref[pl.ds((x * ny + y + k) * 16, 16), :] = whole
                else:
                    n_ref[x, y + k] = whole
                    up_ref[x, y + k] = halves[1]
        if last:
            turn(x)
            if x % GROUP == GROUP - 1:
                for z in range(x - GROUP + 1, x + 1):
                    copy(z).start()

    for x in range(nx):
        plane(x)
    if last:
        for x in range(nx):
            copy(x).wait()
    else:
        emit(nx, ny, place_ref, n_ref, xa_ref, xb_ref, ya_ref, yb_ref)


def ring(axis, by):
    n = lax.axis_size(axis)
    return [(i, (i + by) % n) for i in range(n)]


def pairs(axis):
    n = lax.axis_size(axis)
    first = [(i, i ^ 1) for i in range(n)]
    second = [(i, (i + 1 if i % 2 else i - 1) % n) for i in range(n)]
    return first, second


def exchange(up, xa, xb, ya, yb):
    before = lax.ppermute(up, "tm", ring("tm", 1))
    (x_one, x_two), (y_one, y_two) = pairs("sx"), pairs("sy")
    return (
        before,
        lax.ppermute(xa, "sx", x_one),
        lax.ppermute(xb, "sx", x_two),
        lax.ppermute(yb, "sy", y_two),
        lax.ppermute(ya, "sy", y_one),
    )


def call(kernel, ins, outs, name, scratch=(), flops=10**9, grant=40):
    return pl.pallas_call(
        kernel,
        in_specs=ins,
        out_specs=[VMEM] * len(outs) if len(outs) > 1 else [HBM],
        out_shape=outs,
        scratch_shapes=scratch,
        compiler_params=pltpu.CompilerParams(vmem_limit_bytes=grant * 1024 * 1024),
        cost_estimate=pl.CostEstimate(flops=flops, bytes_accessed=4 * 10**6, transcendentals=0),
        name=name,
    )


def on_device(right_side, current, classes, volume, face_gain, time_gain):
    _, nodes, nx, ny, nz = current.shape
    shape = jax.ShapeDtypeStruct
    faces = [shape((n, 8, nz), F32) for n in (ny, ny, nx, nx)]
    field = shape((nx, ny, nodes, nz), F32)
    half = shape((nx, ny, 8, nz), F32)
    packed = shape((nx, ny, nodes, nz), BF16)
    cube = (nodes, nx * ny, nz)
    r = right_side.reshape(nodes * nx * ny, nz)
    stream = [pltpu.VMEM(cube, F32), pltpu.SemaphoreType.DMA((nx,))]
    cls = classes[0]
    place = jnp.stack([lax.axis_index("tm"), lax.axis_index("sx") % 2, lax.axis_index("sy") % 2])
    place = jnp.broadcast_to(place[:, None, None], (3, 8, nz))
    vol = volume.reshape(volume.shape[0] * nodes, nodes)

    v, *sent = call(
        functools.partial(prep_kernel, nx, ny), [VMEM, HBM], [field, half] + faces, "prep", stream, grant=52
    )(place, current.reshape(cube))
    got = exchange(*sent)
    w, rh, rl = call(
        functools.partial(table_kernel, nx, ny),
        [VMEM] * 5,
        [shape((8 * nodes, 256), BF16), packed, packed],
        "tables", [pltpu.VMEM((128, 128), F32)],
    )(place, vol, face_gain, time_gain.reshape(1, -1), r)
    pack = call(functools.partial(pack_kernel, nx, ny), [VMEM], [packed] * 4, "pack")
    scratch = [pltpu.VMEM((n, 16, nz), BF16) for n in (ny, ny, ny, ny, nx, nx, nx, nx)]
    views = pack(v)
    v, *sent = call(
        functools.partial(sweep_kernel, nx, ny, False),
        [VMEM] * 15, [field, half] + faces, "sweep_a", scratch,
    )(place, w, cls, v, rh, rl, *views, *got)
    got = exchange(*sent)
    views = pack(v)
    (out,) = call(
        functools.partial(sweep_kernel, nx, ny, True),
        [VMEM] * 15, [shape(cube, F32)], "sweep_b", stream + [pltpu.VMEM((nx * ny * nodes, nz), F32)] + scratch,
    )(place, w, cls, v, rh, rl, *views, *got)
    return out.reshape(current.shape)


def solution(mesh):
    placed = (
        P("tm", None, "sx", "sy", None),
        P("tm", None, "sx", "sy", None),
        P("tm", "sx", "sy", None),
        P(),
        P(),
        P(),
    )
    return jax.shard_map(
        on_device,
        mesh=mesh,
        in_specs=placed,
        out_specs=P("tm", None, "sx", "sy", None),
        check_vma=False,
    )
```

time: 41 us -> 32.1 us (0.78)
  Pallas kernels: 12.7 us -> 8.47 us
  starting transfers between devices: 22.2 us -> 19.7 us
  waiting for transfers between devices: 3.89 us -> 2.78 us
  local copies, waits for them, and re-layouts: 1.92 us -> 0.84 us
    pallas_call x4, Pallas kernels: 10.5 us -> 7.25 us  [the longest x1 2.68 us: on_device(): call(functools.partial(sweep_kernel, nx, ny, True), [VMEM] * 15, [shape(c...]
    ppermute x8, starting transfers between devices: 19.4 us -> 16.6 us  [the longest x2 8.34 us: exchange(): lax.ppermute(xb, 'sx', x_two)]
    unnamed x12 -> x10, local copies, waits for them, and re-layouts: 1.91 us -> 0.76 us
    ppermute x8, waiting for transfers between devices: 3.89 us -> 2.77 us  [the longest x2 2.76 us: exchange(): lax.ppermute(yb, 'sy', y_two)]
    pallas_call x2, Pallas kernels: 2.2 us -> 1.22 us  [on_device(): views = pack(v)]
  transfers between devices with their start and end apart: 10 -> 10, of which waited for: 2 -> 1; matrix products, arithmetic and copies ran while one was open for 0% -> 0% of each run, Pallas kernels for 14% -> 8%
where the time goes in v1:
time: 32.1 us; the launch traced here: 32 us
  starting transfers between devices  19.7 us (61%)
  Pallas kernels  8.47 us (26%)
  waiting for transfers between devices  2.78 us (9%)
  local copies, waits for them, and re-layouts  0.84 us (3%)
    ppermute x2, starting transfers between devices, exchange(): lax.ppermute(xb, 'sx', x_two)  8.34 us
    ppermute x2, starting transfers between devices, exchange(): lax.ppermute(yb, 'sy', y_two)  6.41 us
    ppermute x2, starting transfers between devices, exchange(): before = lax.ppermute(up, 'tm', ring('tm', 1))  3.09 us
    ppermute x2, waiting for transfers between devices, exchange(): lax.ppermute(yb, 'sy', y_two)  2.76 us
    pallas_call x1, Pallas kernels, on_device(): call(functools.partial(sweep_kernel, nx, ny, True), [VMEM] * 15, [shape(c...  2.68 us
    pallas_call x1, Pallas kernels, on_device(): call(functools.partial(prep_kernel, nx, ny), [VMEM, HBM], [field, half] +...  1.65 us
    ppermute x2, starting transfers between devices, exchange(): lax.ppermute(xa, 'sx', x_one)  1.64 us
    pallas_call x1, Pallas kernels, on_device(): call(functools.partial(sweep_kernel, nx, ny, False), [VMEM] * 15, [field,...  1.53 us
  transfers between devices with their start and end apart: 10, of which 1 were waited for; matrix products, arithmetic and copies ran while one was open for 0% of the time, Pallas kernels for 8%

profile of v1, /device:TPU:1, one launch (start us, length us, event | category | flops | bytes accessed | tf_op | source)
XLA Modules:
  0.0 32.0 jit_solution(2592946857353588143)
XLA Ops:
  0.0 0.1 pad_add_fusion
  0.1 0.1 broadcast_in_dim.2.place_ref.refs_0_
  0.1 1.6 %prep.1 = (f32[8,16,16,128]{3,2,1,0:T(8,128)S(1)}, f32[8,16,8,128]{3,2,1,0:T(8,128)S(1)}, f32[16,8,128]{2,1,0:T(8,128)S(1)}, f32[16,8,128]{2,1,0:T(8,128)S(1)}, ...) custom-call(s32[3,8,128]{2,1,0:T(8,128)S(1)} %broadcast_in_dim.2.place_ref.refs_0_, f32[16,128,128]{2,1,0:T(8,128)} %bitcast.14), custom_call_target="tpu_custom_call" | custom-call | flops 1000000000 | bytes 4000000 | tf_op jit(solution)/shard_map/prep/pallas_call | solution.py:278
  1.8 2.7 %collective-permute-start = (f32[8,16,8,128]{3,2,1,0:T(8,128)S(1)}, f32[8,16,8,128]{3,2,1,0:T(8,128)S(1)}, u32[]{:S(2)}, u32[]{:S(2)}) collective-permute-start(f32[8,16,8,128]{3,2,1,0:T(8,128)S(1)} %get-tuple-element.36), channel_id=1, source_target_pairs={{0,64},{64,128},{128,192},{192,0},{1,65},{65,129},{129,193},{193,1... | collective-permute-start | bytes 1572872 | tf_op jit(solution)/shard_map/ppermute | solution.py:239
  4.5 4.9 %collective-permute-start.3 = (f32[8,8,128]{2,1,0:T(8,128)S(1)}, f32[8,8,128]{2,1,0:T(8,128)S(1)}, u32[]{:S(2)}, u32[]{:S(2)}) collective-permute-start(f32[8,8,128]{2,1,0:T(8,128)S(1)} %get-tuple-element.39), channel_id=1, source_target_pairs={{0,7},{1,2},{2,1},{3,4},{4,3},{5,6},{6,5},{7,0},{8,15},{9,10},{10,... | collective-permute-start | bytes 98312 | tf_op jit(solution)/shard_map/ppermute | solution.py:245
  9.4 0.0 collective-permute-start.4
  9.4 1.6 %collective-permute-start.1 = (f32[16,8,128]{2,1,0:T(8,128)S(1)}, f32[16,8,128]{2,1,0:T(8,128)S(1)}, u32[]{:S(2)}, u32[]{:S(2)}) collective-permute-start(f32[16,8,128]{2,1,0:T(8,128)S(1)} %get-tuple-element.37), channel_id=1, source_target_pairs={{0,8},{8,0},{16,24},{24,16},{32,40},{40,32},{48,56},{56,48},{1,9},... | collective-permute-start | bytes 196616 | tf_op jit(solution)/shard_map/ppermute | solution.py:243
  11.0 4.7 %collective-permute-start.2 = (f32[16,8,128]{2,1,0:T(8,128)S(1)}, f32[16,8,128]{2,1,0:T(8,128)S(1)}, u32[]{:S(2)}, u32[]{:S(2)}) collective-permute-start(f32[16,8,128]{2,1,0:T(8,128)S(1)} %get-tuple-element.38), channel_id=1, source_target_pairs={{0,56},{8,16},{16,8},{24,32},{32,24},{40,48},{48,40},{56,0},{1,57}... | collective-permute-start | bytes 196616 | tf_op jit(solution)/shard_map/ppermute | solution.py:244
  15.7 0.6 %pack.2 = (bf16[8,16,16,128]{3,2,1,0:T(8,128)(2,1)S(1)}, bf16[8,16,16,128]{3,2,1,0:T(8,128)(2,1)S(1)}, bf16[8,16,16,128]{3,2,1,0:T(8,128)(2,1)S(1)}, bf16[8,16,16,128]{3,2,1,0:T(8,128)(2,1)S(1)}) custom-call(f32[8,16,16,128]{3,2,1,0:T(8,128)S(1)} %get-tuple-element.29.v_ref.refs_3_), custom_call_target="tpu_custom_call" | custom-call | flops 1000000000 | bytes 4000000 | tf_op jit(solution)/shard_map/pack/pallas_call | solution.py:290
  16.3 0.0 copy-start.4
  16.3 0.6 %copy-done.1 = f32[1,16,8,16,128]{4,3,2,1,0:T(8,128)S(1)} copy-done((f32[1,16,8,16,128]{4,3,2,1,0:T(8,128)S(1)}, f32[1,16,8,16,128]{4,3,2,1,0:T(8,128)}, u32[]{:S(2)}) %copy-start.1) | copy-done | bytes 1048600
  16.9 0.0 copy-done.2
  16.9 0.2 copy-done.3
  17.1 1.4 %tables.1 = (bf16[128,256]{1,0:T(8,128)(2,1)S(1)}, bf16[8,16,16,128]{3,2,1,0:T(8,128)(2,1)S(1)}, bf16[8,16,16,128]{3,2,1,0:T(8,128)(2,1)S(1)}) custom-call(s32[3,8,128]{2,1,0:T(8,128)S(1)} %broadcast_in_dim.2.place_ref.refs_0_, f32[128,16]{1,0:T(8,128)S(1)} %bitcast.12, f32[8,6]{1,0:T(8,128)S(1)} %copy-done.3, f32[1,8]{1,0:T(1,128)S(1)} %bitcast.13, ...), custom_call_target="tpu_custom_call" | custom-call | flops 1000000000 | bytes 4000000 | tf_op jit(solution)/shard_map/tables/pallas_call | solution.py:282
  18.5 0.0 collective-permute-done.3.refs_13_
  18.5 0.0 collective-permute-done.4.refs_14_
  18.5 0.0 collective-permute-done.1.refs_11_
  18.5 0.0 collective-permute-done.2.refs_12_
  18.5 0.0 collective-permute-done.refs_10_
  18.5 1.5 %sweep_a.1 = (f32[8,16,16,128]{3,2,1,0:T(8,128)S(1)}, f32[8,16,8,128]{3,2,1,0:T(8,128)S(1)}, f32[16,8,128]{2,1,0:T(8,128)S(1)}, f32[16,8,128]{2,1,0:T(8,128)S(1)...) custom-call(s32[3,8,128]{2,1,0:T(8,128)S(1)} %broadcast_in_dim.2.place_ref.refs_0_, ...), custom_call_target="tpu_custom_call" | custom-call | flops 1000000000 | bytes 4000000 | tf_op jit(solution)/shard_map/sweep_a/pallas_call | solution.py:291
  20.1 0.4 %collective-permute-start.5 = (f32[8,16,8,128]{3,2,1,0:T(8,128)S(1)}, f32[8,16,8,128]{3,2,1,0:T(8,128)S(1)}, u32[]{:S(2)}, u32[]{:S(2)}) collective-permute-start(f32[8,16,8,128]{3,2,1,0:T(8,128)S(1)} %get-tuple-element.46), channel_id=1, source_target_pairs={{0,64},{64,128},{128,192},{192,0},{1,65},{65,129},{129,193},{193,1... | collective-permute-start | bytes 1572872 | tf_op jit(solution)/shard_map/ppermute | solution.py:239
  20.5 1.5 %collective-permute-start.8 = (f32[8,8,128]{2,1,0:T(8,128)S(1)}, f32[8,8,128]{2,1,0:T(8,128)S(1)}, u32[]{:S(2)}, u32[]{:S(2)}) collective-permute-start(f32[8,8,128]{2,1,0:T(8,128)S(1)} %get-tuple-element.49), channel_id=1, source_target_pairs={{0,7},{1,2},{2,1},{3,4},{4,3},{5,6},{6,5},{7,0},{8,15},{9,10},{10,... | collective-permute-start | bytes 98312 | tf_op jit(solution)/shard_map/ppermute | solution.py:245
  22.0 0.2 collective-permute-start.9
  22.2 0.0 collective-permute-start.6
  22.2 3.7 %collective-permute-start.7 = (f32[16,8,128]{2,1,0:T(8,128)S(1)}, f32[16,8,128]{2,1,0:T(8,128)S(1)}, u32[]{:S(2)}, u32[]{:S(2)}) collective-permute-start(f32[16,8,128]{2,1,0:T(8,128)S(1)} %get-tuple-element.48), channel_id=1, source_target_pairs={{0,56},{8,16},{16,8},{24,32},{32,24},{40,48},{48,40},{56,0},{1,57}... | collective-permute-start | bytes 196616 | tf_op jit(solution)/shard_map/ppermute | solution.py:244
  25.9 0.6 %pack.3 = (bf16[8,16,16,128]{3,2,1,0:T(8,128)(2,1)S(1)}, bf16[8,16,16,128]{3,2,1,0:T(8,128)(2,1)S(1)}, bf16[8,16,16,128]{3,2,1,0:T(8,128)(2,1)S(1)}, bf16[8,16,16,128]{3,2,1,0:T(8,128)(2,1)S(1)}) custom-call(f32[8,16,16,128]{3,2,1,0:T(8,128)S(1)} %get-tuple-element.41.v_ref.refs_3_), custom_call_target="tpu_custom_call" | custom-call | flops 1000000000 | bytes 4000000 | tf_op jit(solution)/shard_map/pack/pallas_call | solution.py:296
  26.5 2.8 %collective-permute-done.8.refs_13_ = f32[8,8,128]{2,1,0:T(8,128)S(1)} collective-permute-done((f32[8,8,128]{2,1,0:T(8,128)S(1)}, f32[8,8,128]{2,1,0:T(8,128)S(1)}, u32[]{:S(2)}, u32[]{:S(2)}) %collective-permute-start.8) | collective-permute-done | bytes 32800 | tf_op jit(solution)/shard_map/ppermute | solution.py:245
  29.3 0.0 collective-permute-done.9.refs_14_
  29.3 0.0 collective-permute-done.6.refs_11_
  29.3 0.0 collective-permute-done.7.refs_12_
  29.3 0.0 collective-permute-done.5.refs_10_
  29.3 2.7 %sweep_b.1 = f32[16,128,128]{2,1,0:T(8,128)} custom-call(s32[3,8,128]{2,1,0:T(8,128)S(1)} %broadcast_in_dim.2.place_ref.refs_0_, bf16[128,256]{1,0:T(8,128)(2,1)S(1)} %get-tuple-element.28.refs_1_, s32[8,16,128]{2,1,0:T(8,128)S(1)} %bitcast.10, f32[8,16,16,128]{3,2,1,0:T(8,128)S(1)} %get-tuple-element.41.v_ref.refs_3_, ...), custom_call_target="tpu_custom_call" | custom-call | flops 1000000000 | bytes 4000000 | tf_op jit(solution)/shard_map/sweep_b/pallas_call | solution.py:297
  (6 shorter events, 0.0 us)
Async XLA Ops:
  1.8 16.7 %collective-permute-start = (f32[8,16,8,128]{3,2,1,0:T(8,128)S(1)}, f32[8,16,8,128]{3,2,1,0:T(8,128)S(1)}, u32[]{:S(2)}, u32[]{:S(2)}) collective-permute-start(f32[8,16,8,128]{3,2,1,0:T(8,128)S(1)} %get-tuple-element.36), channel_id=1, source_target_pairs={{0,64},{64,128},{128,192},{192,0},{1,65},{65,129},{129,193},{193,1... | collective-permute-start | bytes 1572872 | tf_op jit(solution)/shard_map/ppermute | solution.py:239
  4.5 14.0 %collective-permute-start.3 = (f32[8,8,128]{2,1,0:T(8,128)S(1)}, f32[8,8,128]{2,1,0:T(8,128)S(1)}, u32[]{:S(2)}, u32[]{:S(2)}) collective-permute-start(f32[8,8,128]{2,1,0:T(8,128)S(1)} %get-tuple-element.39), channel_id=1, source_target_pairs={{0,7},{1,2},{2,1},{3,4},{4,3},{5,6},{6,5},{7,0},{8,15},{9,10},{10,... | collective-permute-start | bytes 98312 | tf_op jit(solution)/shard_map/ppermute | solution.py:245
  9.4 9.1 %collective-permute-start.4 = (f32[8,8,128]{2,1,0:T(8,128)S(1)}, f32[8,8,128]{2,1,0:T(8,128)S(1)}, u32[]{:S(2)}, u32[]{:S(2)}) collective-permute-start(f32[8,8,128]{2,1,0:T(8,128)S(1)} %get-tuple-element.40), channel_id=1, source_target_pairs={{0,1},{1,0},{2,3},{3,2},{4,5},{5,4},{6,7},{7,6},{8,9},{9,8},{10,11... | collective-permute-start | bytes 98312 | tf_op jit(solution)/shard_map/ppermute | solution.py:246
  9.4 9.1 %collective-permute-start.1 = (f32[16,8,128]{2,1,0:T(8,128)S(1)}, f32[16,8,128]{2,1,0:T(8,128)S(1)}, u32[]{:S(2)}, u32[]{:S(2)}) collective-permute-start(f32[16,8,128]{2,1,0:T(8,128)S(1)} %get-tuple-element.37), channel_id=1, source_target_pairs={{0,8},{8,0},{16,24},{24,16},{32,40},{40,32},{48,56},{56,48},{1,9},... | collective-permute-start | bytes 196616 | tf_op jit(solution)/shard_map/ppermute | solution.py:243
  11.0 7.5 %collective-permute-start.2 = (f32[16,8,128]{2,1,0:T(8,128)S(1)}, f32[16,8,128]{2,1,0:T(8,128)S(1)}, u32[]{:S(2)}, u32[]{:S(2)}) collective-permute-start(f32[16,8,128]{2,1,0:T(8,128)S(1)} %get-tuple-element.38), channel_id=1, source_target_pairs={{0,56},{8,16},{16,8},{24,32},{32,24},{40,48},{48,40},{56,0},{1,57}... | collective-permute-start | bytes 196616 | tf_op jit(solution)/shard_map/ppermute | solution.py:244
  15.7 1.2 %copy-start.1 = (f32[1,16,8,16,128]{4,3,2,1,0:T(8,128)S(1)}, f32[1,16,8,16,128]{4,3,2,1,0:T(8,128)}, u32[]{:S(2)}) copy-start(f32[1,16,8,16,128]{4,3,2,1,0:T(8,128)} %param.6) | copy-start | bytes 3145732
  15.7 1.2 %copy-start.2 = (f32[8,16,16]{2,1,0:T(8,128)S(1)}, f32[8,16,16]{2,1,0:T(8,128)}, u32[]{:S(2)}) copy-start(f32[8,16,16]{2,1,0:T(8,128)} %param.9) | copy-start | bytes 24580
  16.3 0.8 %copy-start.3 = (f32[8,6]{1,0:T(8,128)S(1)}, f32[8,6]{1,0:T(8,128)}, u32[]{:S(2)}) copy-start(f32[8,6]{1,0:T(8,128)} %face_ref.1) | copy-start | bytes 580
  16.3 0.8 %copy-start.4 = (f32[8]{0:T(128)S(1)}, f32[8]{0:T(128)}, u32[]{:S(2)}) copy-start(f32[8]{0:T(128)} %param.11) | copy-start | bytes 100
  17.1 1.5 %copy-start = (s32[1,8,16,128]{3,2,1,0:T(8,128)S(1)}, s32[1,8,16,128]{3,2,1,0:T(8,128)}, u32[]{:S(2)}) copy-start(s32[1,8,16,128]{3,2,1,0:T(8,128)} %param.8) | copy-start | bytes 196612
  20.1 9.2 %collective-permute-start.5 = (f32[8,16,8,128]{3,2,1,0:T(8,128)S(1)}, f32[8,16,8,128]{3,2,1,0:T(8,128)S(1)}, u32[]{:S(2)}, u32[]{:S(2)}) collective-permute-start(f32[8,16,8,128]{3,2,1,0:T(8,128)S(1)} %get-tuple-element.46), channel_id=1, source_target_pairs={{0,64},{64,128},{128,192},{192,0},{1,65},{65,129},{129,193},{193,1... | collective-permute-start | bytes 1572872 | tf_op jit(solution)/shard_map/ppermute | solution.py:239
  20.5 8.8 %collective-permute-start.8 = (f32[8,8,128]{2,1,0:T(8,128)S(1)}, f32[8,8,128]{2,1,0:T(8,128)S(1)}, u32[]{:S(2)}, u32[]{:S(2)}) collective-permute-start(f32[8,8,128]{2,1,0:T(8,128)S(1)} %get-tuple-element.49), channel_id=1, source_target_pairs={{0,7},{1,2},{2,1},{3,4},{4,3},{5,6},{6,5},{7,0},{8,15},{9,10},{10,... | collective-permute-start | bytes 98312 | tf_op jit(solution)/shard_map/ppermute | solution.py:245
  22.0 7.3 %collective-permute-start.9 = (f32[8,8,128]{2,1,0:T(8,128)S(1)}, f32[8,8,128]{2,1,0:T(8,128)S(1)}, u32[]{:S(2)}, u32[]{:S(2)}) collective-permute-start(f32[8,8,128]{2,1,0:T(8,128)S(1)} %get-tuple-element.50), channel_id=1, source_target_pairs={{0,1},{1,0},{2,3},{3,2},{4,5},{5,4},{6,7},{7,6},{8,9},{9,8},{10,11... | collective-permute-start | bytes 98312 | tf_op jit(solution)/shard_map/ppermute | solution.py:246
  22.2 7.0 %collective-permute-start.6 = (f32[16,8,128]{2,1,0:T(8,128)S(1)}, f32[16,8,128]{2,1,0:T(8,128)S(1)}, u32[]{:S(2)}, u32[]{:S(2)}) collective-permute-start(f32[16,8,128]{2,1,0:T(8,128)S(1)} %get-tuple-element.47), channel_id=1, source_target_pairs={{0,8},{8,0},{16,24},{24,16},{32,40},{40,32},{48,56},{56,48},{1,9},... | collective-permute-start | bytes 196616 | tf_op jit(solution)/shard_map/ppermute | solution.py:243
  22.2 7.0 %collective-permute-start.7 = (f32[16,8,128]{2,1,0:T(8,128)S(1)}, f32[16,8,128]{2,1,0:T(8,128)S(1)}, u32[]{:S(2)}, u32[]{:S(2)}) collective-permute-start(f32[16,8,128]{2,1,0:T(8,128)S(1)} %get-tuple-element.48), channel_id=1, source_target_pairs={{0,56},{8,16},{16,8},{24,32},{32,24},{40,48},{48,40},{56,0},{1,57}... | collective-permute-start | bytes 196616 | tf_op jit(solution)/shard_map/ppermute | solution.py:244

commit v2 on v1

--- a/solution.py
+++ b/solution.py
@@ -9,7 +9,6 @@
 F32 = jnp.float32
 BF16 = jnp.bfloat16
 DAMP = 0.7
-GROUP = 4
 VMEM = pl.BlockSpec(memory_space=pltpu.VMEM)
 HBM = pl.BlockSpec(memory_space=pltpu.HBM)
 
@@ -79,6 +78,14 @@
             uh_ref[x, y], ul_ref[x, y] = split2(u)
             mixed = jnp.where(odd, pltpu.roll(u, 1, 1), pltpu.roll(u, 127, 1))
             zh_ref[x, y], zl_ref[x, y] = split2(mixed)
+
+
+def both_kernel(nx, ny, v_ref, r_ref, uh_ref, ul_ref, zh_ref, zl_ref, rh_ref, rl_ref):
+    pack_kernel(nx, ny, v_ref, uh_ref, ul_ref, zh_ref, zl_ref)
+    for x in range(nx):
+        for y in range(ny):
+            r = r_ref[pl.ds(x * ny + y, 16, stride=nx * ny), :]
+            rh_ref[x, y], rl_ref[x, y] = split2(r)
 
 
 def inverses(vol_ref, wide_ref):
@@ -102,7 +109,7 @@
     return jnp.transpose(jnp.concatenate([total, jnp.zeros((112, 128), F32)], axis=0))
 
 
-def table_kernel(nx, ny, place_ref, vol_ref, face_ref, time_ref, r_ref, w_ref, rh_ref, rl_ref, wide_ref):
+def table_kernel(place_ref, vol_ref, face_ref, time_ref, w_ref, wide_ref):
     classes = face_ref.shape[0]
     lane = lax.broadcasted_iota(jnp.int32, (16, 128), 1)
     inverse = inverses(vol_ref, wide_ref)
@@ -127,11 +134,6 @@
         second = lo + pltpu.roll(thi, 64, 1) + pltpu.roll(thi, 72, 1)
         second = second + pltpu.roll(tlo, 80, 1) + pltpu.roll(tlo, 88, 1)
         w_ref[rows, 128:256] = second.astype(BF16)
-
-    for x in range(nx):
-        for y in range(ny):
-            r = r_ref[pl.ds(x * ny + y, 16, stride=nx * ny), :]
-            rh_ref[x, y], rl_ref[x, y] = split2(r)
 
 
 def sweep_kernel(nx, ny, last, *refs):
@@ -210,8 +212,8 @@
                     up_ref[x, y + k] = halves[1]
         if last:
             turn(x)
-            if x % GROUP == GROUP - 1:
-                for z in range(x - GROUP + 1, x + 1):
+            if x in (nx // 2, nx - 1):
+                for z in range(nx // 2 + 1) if x == nx // 2 else range(nx // 2 + 1, nx):
                     copy(z).start()
 
     for x in range(nx):
@@ -247,11 +249,11 @@
     )
 
 
-def call(kernel, ins, outs, name, scratch=(), flops=10**9, grant=40):
+def call(kernel, ins, outs, name, scratch=(), flops=10**9, grant=40, streamed=False):
     return pl.pallas_call(
         kernel,
         in_specs=ins,
-        out_specs=[VMEM] * len(outs) if len(outs) > 1 else [HBM],
+        out_specs=[HBM if streamed else VMEM] * len(outs),
         out_shape=outs,
         scratch_shapes=scratch,
         compiler_params=pltpu.CompilerParams(vmem_limit_bytes=grant * 1024 * 1024),
@@ -271,23 +273,23 @@
     r = right_side.reshape(nodes * nx * ny, nz)
     stream = [pltpu.VMEM(cube, F32), pltpu.SemaphoreType.DMA((nx,))]
     cls = classes[0]
-    place = jnp.stack([lax.axis_index("tm"), lax.axis_index("sx") % 2, lax.axis_index("sy") % 2])
-    place = jnp.broadcast_to(place[:, None, None], (3, 8, nz))
+    which = lax.broadcasted_iota(jnp.int32, (3, 8, nz), 0)
+    odd_x, odd_y = lax.axis_index("sx") % 2, lax.axis_index("sy") % 2
+    place = jnp.where(which == 0, lax.axis_index("tm"), jnp.where(which == 1, odd_x, odd_y))
     vol = volume.reshape(volume.shape[0] * nodes, nodes)
 
     v, *sent = call(
         functools.partial(prep_kernel, nx, ny), [VMEM, HBM], [field, half] + faces, "prep", stream, grant=52
     )(place, current.reshape(cube))
     got = exchange(*sent)
-    w, rh, rl = call(
-        functools.partial(table_kernel, nx, ny),
-        [VMEM] * 5,
-        [shape((8 * nodes, 256), BF16), packed, packed],
-        "tables", [pltpu.VMEM((128, 128), F32)],
-    )(place, vol, face_gain, time_gain.reshape(1, -1), r)
+    (w,) = call(
+        table_kernel, [VMEM] * 4, [shape((8 * nodes, 256), BF16)], "tables", [pltpu.VMEM((128, 128), F32)]
+    )(place, vol, face_gain, time_gain.reshape(1, -1))
+    *views, rh, rl = call(
+        functools.partial(both_kernel, nx, ny), [VMEM] * 2, [packed] * 6, "both"
+    )(v, r)
     pack = call(functools.partial(pack_kernel, nx, ny), [VMEM], [packed] * 4, "pack")
     scratch = [pltpu.VMEM((n, 16, nz), BF16) for n in (ny, ny, ny, ny, nx, nx, nx, nx)]
-    views = pack(v)
     v, *sent = call(
         functools.partial(sweep_kernel, nx, ny, False),
         [VMEM] * 15, [field, half] + faces, "sweep_a", scratch,
@@ -296,7 +298,7 @@
     views = pack(v)
     (out,) = call(
         functools.partial(sweep_kernel, nx, ny, True),
-        [VMEM] * 15, [shape(cube, F32)], "sweep_b", stream + [pltpu.VMEM((nx * ny * nodes, nz), F32)] + scratch,
+        [VMEM] * 15, [shape(cube, F32)], "sweep_b", stream + [pltpu.VMEM((nx * ny * nodes, nz), F32)] + scratch, streamed=True,
     )(place, w, cls, v, rh, rl, *views, *got)
     return out.reshape(current.shape)
 

time: 32.1 us -> 32 us (level)
    pallas_call x2 -> x1, Pallas kernels: 1.22 us -> 0.61 us  [on_device(): views = pack(v)]
    pallas_call x1 -> x2, Pallas kernels: 1.4 us -> 1.99 us  [the longest x1 1.14 us: on_device(): call(functools.partial(both_kernel, nx, ny), [VMEM] * 2, [packed] * 6, 'b...]
where the time goes in v2:
time: 32 us; the launch traced here: 31.9 us
  starting transfers between devices  19.9 us (62%)
  Pallas kernels  8.58 us (27%)
  waiting for transfers between devices  2.63 us (8%)
  local copies, waits for them, and re-layouts  0.65 us (2%)
    ppermute x2, starting transfers between devices, exchange(): lax.ppermute(xb, 'sx', x_two)  8.49 us
    ppermute x2, starting transfers between devices, exchange(): lax.ppermute(yb, 'sy', y_two)  6.42 us
    ppermute x2, starting transfers between devices, exchange(): before = lax.ppermute(up, 'tm', ring('tm', 1))  3.09 us
    pallas_call x1, Pallas kernels, on_device(): call(functools.partial(sweep_kernel, nx, ny, True), [VMEM] * 15, [shape(c...  2.69 us
    ppermute x2, waiting for transfers between devices, exchange(): lax.ppermute(yb, 'sy', y_two)  2.61 us
    pallas_call x1, Pallas kernels, on_device(): call(functools.partial(prep_kernel, nx, ny), [VMEM, HBM], [field, half] +...  1.74 us
    ppermute x2, starting transfers between devices, exchange(): lax.ppermute(xa, 'sx', x_one)  1.64 us
    pallas_call x1, Pallas kernels, on_device(): call(functools.partial(sweep_kernel, nx, ny, False), [VMEM] * 15, [field,...  1.56 us
  transfers between devices with their start and end apart: 10, of which 1 were waited for; matrix products, arithmetic and copies ran while one was open for 0% of the time, Pallas kernels for 8%

profile of v2, /device:TPU:1, one launch (start us, length us, event | category | flops | bytes accessed | tf_op | source)
XLA Modules:
  0.0 31.9 jit_solution(12407937118707090051)
XLA Ops:
  0.0 0.1 broadcast_select_fusion.place_ref.refs_0_
  0.1 1.7 %prep.1 = (f32[8,16,16,128]{3,2,1,0:T(8,128)S(1)}, f32[8,16,8,128]{3,2,1,0:T(8,128)S(1)}, f32[16,8,128]{2,1,0:T(8,128)S(1)}, f32[16,8,128]{2,1,0:T(8,128)S(1)}, ...) custom-call(s32[3,8,128]{2,1,0:T(8,128)S(1)} %broadcast_select_fusion.place_ref.refs_0_, f32[16,128,128]{2,1,0:T(8,128)} %bitcast.11), custom_call_target="tpu_custom_call" | custom-call | flops 1000000000 | bytes 4000000 | tf_op jit(solution)/shard_map/prep/pallas_call | solution.py:281
  1.8 2.7 %collective-permute-start = (f32[8,16,8,128]{3,2,1,0:T(8,128)S(1)}, f32[8,16,8,128]{3,2,1,0:T(8,128)S(1)}, u32[]{:S(2)}, u32[]{:S(2)}) collective-permute-start(f32[8,16,8,128]{3,2,1,0:T(8,128)S(1)} %get-tuple-element.34), channel_id=1, source_target_pairs={{0,64},{64,128},{128,192},{192,0},{1,65},{65,129},{129,193},{193,1... | collective-permute-start | bytes 1572872 | tf_op jit(solution)/shard_map/ppermute | solution.py:241
  4.5 4.9 %collective-permute-start.3 = (f32[8,8,128]{2,1,0:T(8,128)S(1)}, f32[8,8,128]{2,1,0:T(8,128)S(1)}, u32[]{:S(2)}, u32[]{:S(2)}) collective-permute-start(f32[8,8,128]{2,1,0:T(8,128)S(1)} %get-tuple-element.37), channel_id=1, source_target_pairs={{0,7},{1,2},{2,1},{3,4},{4,3},{5,6},{6,5},{7,0},{8,15},{9,10},{10,... | collective-permute-start | bytes 98312 | tf_op jit(solution)/shard_map/ppermute | solution.py:247
  9.4 0.0 collective-permute-start.4
  9.4 1.6 %collective-permute-start.1 = (f32[16,8,128]{2,1,0:T(8,128)S(1)}, f32[16,8,128]{2,1,0:T(8,128)S(1)}, u32[]{:S(2)}, u32[]{:S(2)}) collective-permute-start(f32[16,8,128]{2,1,0:T(8,128)S(1)} %get-tuple-element.35), channel_id=1, source_target_pairs={{0,8},{8,0},{16,24},{24,16},{32,40},{40,32},{48,56},{56,48},{1,9},... | collective-permute-start | bytes 196616 | tf_op jit(solution)/shard_map/ppermute | solution.py:245
  11.1 4.7 %collective-permute-start.2 = (f32[16,8,128]{2,1,0:T(8,128)S(1)}, f32[16,8,128]{2,1,0:T(8,128)S(1)}, u32[]{:S(2)}, u32[]{:S(2)}) collective-permute-start(f32[16,8,128]{2,1,0:T(8,128)S(1)} %get-tuple-element.36), channel_id=1, source_target_pairs={{0,56},{8,16},{16,8},{24,32},{32,24},{40,48},{48,40},{56,0},{1,57}... | collective-permute-start | bytes 196616 | tf_op jit(solution)/shard_map/ppermute | solution.py:246
  15.7 0.0 copy-done.1
  15.7 1.1 %both.1 = (bf16[8,16,16,128]{3,2,1,0:T(8,128)(2,1)S(1)}, bf16[8,16,16,128]{3,2,1,0:T(8,128)(2,1)S(1)}, bf16[8,16,16,128]{3,2,1,0:T(8,128)(2,1)S(1)}, bf16[8,16,1...) custom-call(f32[8,16,16,128]{3,2,1,0:T(8,128)S(1)} %get-tuple-element.27.v_ref., ...), custom_call_target="tpu_custom_call" | custom-call | flops 1000000000 | bytes 4000000 | tf_op jit(solution)/shard_map/both/pallas_call | solution.py:288
  16.9 0.0 copy-start.4
  16.9 0.0 copy-done.2
  16.9 0.6 %copy-done.4 = f32[8]{0:T(128)S(1)} copy-done((f32[8]{0:T(128)S(1)}, f32[8]{0:T(128)}, u32[]{:S(2)}) %copy-start.4) | copy-done | bytes 56
  17.5 0.8 %tables.1.refs_1_ = bf16[128,256]{1,0:T(8,128)(2,1)S(1)} custom-call(s32[3,8,128]{2,1,0:T(8,128)S(1)} %broadcast_select_fusion.place_ref.refs_0_, f32[128,16]{1,0:T(8,128)S(1)} %bitcast.9, f32[8,6]{1,0:T(8,128)S(1)} %copy-done.3, f32[1,8]{1,0:T(1,128)S(1)} %bitcast.10), custom_call_target="tpu_custom_call" | custom-call | flops 1000000000 | bytes 4000000 | tf_op jit(solution)/shard_map/tables/pallas_call | solution.py:285
  18.4 0.0 collective-permute-done.3.refs_13_
  18.4 0.0 collective-permute-done.4.refs_14_
  18.4 0.0 collective-permute-done.1.refs_11_
  18.4 0.0 collective-permute-done.2.refs_12_
  18.4 0.0 collective-permute-done.refs_10_
  18.4 0.0 copy-done
  18.4 1.6 %sweep_a.1 = (f32[8,16,16,128]{3,2,1,0:T(8,128)S(1)}, f32[8,16,8,128]{3,2,1,0:T(8,128)S(1)}, f32[16,8,128]{2,1,0:T(8,128)S(1)}, f32[16,8,128]{2,1,0:T(8,128)S(1)...) custom-call(s32[3,8,128]{2,1,0:T(8,128)S(1)} %broadcast_select_fusion.place_ref.refs_0_, ...), custom_call_target="tpu_custom_call" | custom-call | flops 1000000000 | bytes 4000000 | tf_op jit(solution)/shard_map/sweep_a/pallas_call | solution.py:293
  20.0 0.4 %collective-permute-start.5 = (f32[8,16,8,128]{3,2,1,0:T(8,128)S(1)}, f32[8,16,8,128]{3,2,1,0:T(8,128)S(1)}, u32[]{:S(2)}, u32[]{:S(2)}) collective-permute-start(f32[8,16,8,128]{3,2,1,0:T(8,128)S(1)} %get-tuple-element.44), channel_id=1, source_target_pairs={{0,64},{64,128},{128,192},{192,0},{1,65},{65,129},{129,193},{193,1... | collective-permute-start | bytes 1572872 | tf_op jit(solution)/shard_map/ppermute | solution.py:241
  20.4 1.5 %collective-permute-start.8 = (f32[8,8,128]{2,1,0:T(8,128)S(1)}, f32[8,8,128]{2,1,0:T(8,128)S(1)}, u32[]{:S(2)}, u32[]{:S(2)}) collective-permute-start(f32[8,8,128]{2,1,0:T(8,128)S(1)} %get-tuple-element.47), channel_id=1, source_target_pairs={{0,7},{1,2},{2,1},{3,4},{4,3},{5,6},{6,5},{7,0},{8,15},{9,10},{10,... | collective-permute-start | bytes 98312 | tf_op jit(solution)/shard_map/ppermute | solution.py:247
  21.9 0.2 collective-permute-start.9
  22.2 0.0 collective-permute-start.6
  22.2 3.8 %collective-permute-start.7 = (f32[16,8,128]{2,1,0:T(8,128)S(1)}, f32[16,8,128]{2,1,0:T(8,128)S(1)}, u32[]{:S(2)}, u32[]{:S(2)}) collective-permute-start(f32[16,8,128]{2,1,0:T(8,128)S(1)} %get-tuple-element.46), channel_id=1, source_target_pairs={{0,56},{8,16},{16,8},{24,32},{32,24},{40,48},{48,40},{56,0},{1,57}... | collective-permute-start | bytes 196616 | tf_op jit(solution)/shard_map/ppermute | solution.py:246
  26.0 0.6 %pack.1 = (bf16[8,16,16,128]{3,2,1,0:T(8,128)(2,1)S(1)}, bf16[8,16,16,128]{3,2,1,0:T(8,128)(2,1)S(1)}, bf16[8,16,16,128]{3,2,1,0:T(8,128)(2,1)S(1)}, bf16[8,16,16,128]{3,2,1,0:T(8,128)(2,1)S(1)}) custom-call(f32[8,16,16,128]{3,2,1,0:T(8,128)S(1)} %get-tuple-element.39.v_ref.refs_3_), custom_call_target="tpu_custom_call" | custom-call | flops 1000000000 | bytes 4000000 | tf_op jit(solution)/shard_map/pack/pallas_call | solution.py:298
  26.6 2.6 %collective-permute-done.8.refs_13_ = f32[8,8,128]{2,1,0:T(8,128)S(1)} collective-permute-done((f32[8,8,128]{2,1,0:T(8,128)S(1)}, f32[8,8,128]{2,1,0:T(8,128)S(1)}, u32[]{:S(2)}, u32[]{:S(2)}) %collective-permute-start.8) | collective-permute-done | bytes 32800 | tf_op jit(solution)/shard_map/ppermute | solution.py:247
  29.2 0.0 collective-permute-done.9.refs_14_
  29.2 0.0 collective-permute-done.6.refs_11_
  29.2 0.0 collective-permute-done.7.refs_12_
  29.2 0.0 collective-permute-done.5.refs_10_
  29.2 2.7 %sweep_b.1 = f32[16,128,128]{2,1,0:T(8,128)} custom-call(s32[3,8,128]{2,1,0:T(8,128)S(1)} %broadcast_select_fusion.place_ref.refs_0_, bf16[128,256]{1,0:T(8,128)(2,1)S(1)} %tables.1.refs_1_, s32[8,16,128]{2,1,0:T(8,128)S(1)} %bitcast.7, f32[8,16,16,128]{3,2,1,0:T(8,128)S(1)} %get-tuple-element.39.v_ref.refs_3_, ...), custom_call_target="tpu_custom_call" | custom-call | flops 1000000000 | bytes 4000000 | tf_op jit(solution)/shard_map/sweep_b/pallas_call | solution.py:299
  (7 shorter events, 0.0 us)
Async XLA Ops:
  0.1 15.6 %copy-start.1 = (f32[1,16,8,16,128]{4,3,2,1,0:T(8,128)S(1)}, f32[1,16,8,16,128]{4,3,2,1,0:T(8,128)}, u32[]{:S(2)}) copy-start(f32[1,16,8,16,128]{4,3,2,1,0:T(8,128)} %param.6) | copy-start | bytes 3145732
  1.8 16.6 %collective-permute-start = (f32[8,16,8,128]{3,2,1,0:T(8,128)S(1)}, f32[8,16,8,128]{3,2,1,0:T(8,128)S(1)}, u32[]{:S(2)}, u32[]{:S(2)}) collective-permute-start(f32[8,16,8,128]{3,2,1,0:T(8,128)S(1)} %get-tuple-element.34), channel_id=1, source_target_pairs={{0,64},{64,128},{128,192},{192,0},{1,65},{65,129},{129,193},{193,1... | collective-permute-start | bytes 1572872 | tf_op jit(solution)/shard_map/ppermute | solution.py:241
  4.5 13.9 %collective-permute-start.3 = (f32[8,8,128]{2,1,0:T(8,128)S(1)}, f32[8,8,128]{2,1,0:T(8,128)S(1)}, u32[]{:S(2)}, u32[]{:S(2)}) collective-permute-start(f32[8,8,128]{2,1,0:T(8,128)S(1)} %get-tuple-element.37), channel_id=1, source_target_pairs={{0,7},{1,2},{2,1},{3,4},{4,3},{5,6},{6,5},{7,0},{8,15},{9,10},{10,... | collective-permute-start | bytes 98312 | tf_op jit(solution)/shard_map/ppermute | solution.py:247
  9.4 9.0 %collective-permute-start.4 = (f32[8,8,128]{2,1,0:T(8,128)S(1)}, f32[8,8,128]{2,1,0:T(8,128)S(1)}, u32[]{:S(2)}, u32[]{:S(2)}) collective-permute-start(f32[8,8,128]{2,1,0:T(8,128)S(1)} %get-tuple-element.38), channel_id=1, source_target_pairs={{0,1},{1,0},{2,3},{3,2},{4,5},{5,4},{6,7},{7,6},{8,9},{9,8},{10,11... | collective-permute-start | bytes 98312 | tf_op jit(solution)/shard_map/ppermute | solution.py:248
  9.4 9.0 %collective-permute-start.1 = (f32[16,8,128]{2,1,0:T(8,128)S(1)}, f32[16,8,128]{2,1,0:T(8,128)S(1)}, u32[]{:S(2)}, u32[]{:S(2)}) collective-permute-start(f32[16,8,128]{2,1,0:T(8,128)S(1)} %get-tuple-element.35), channel_id=1, source_target_pairs={{0,8},{8,0},{16,24},{24,16},{32,40},{40,32},{48,56},{56,48},{1,9},... | collective-permute-start | bytes 196616 | tf_op jit(solution)/shard_map/ppermute | solution.py:245
  11.1 7.3 %collective-permute-start.2 = (f32[16,8,128]{2,1,0:T(8,128)S(1)}, f32[16,8,128]{2,1,0:T(8,128)S(1)}, u32[]{:S(2)}, u32[]{:S(2)}) collective-permute-start(f32[16,8,128]{2,1,0:T(8,128)S(1)} %get-tuple-element.36), channel_id=1, source_target_pairs={{0,56},{8,16},{16,8},{24,32},{32,24},{40,48},{48,40},{56,0},{1,57}... | collective-permute-start | bytes 196616 | tf_op jit(solution)/shard_map/ppermute | solution.py:246
  15.7 1.2 %copy-start.2 = (f32[8,16,16]{2,1,0:T(8,128)S(1)}, f32[8,16,16]{2,1,0:T(8,128)}, u32[]{:S(2)}) copy-start(f32[8,16,16]{2,1,0:T(8,128)} %param.9) | copy-start | bytes 24580
  15.7 1.2 %copy-start.3 = (f32[8,6]{1,0:T(8,128)S(1)}, f32[8,6]{1,0:T(8,128)}, u32[]{:S(2)}) copy-start(f32[8,6]{1,0:T(8,128)} %face_ref.1) | copy-start | bytes 580
  16.9 0.7 %copy-start.4 = (f32[8]{0:T(128)S(1)}, f32[8]{0:T(128)}, u32[]{:S(2)}) copy-start(f32[8]{0:T(128)} %param.11) | copy-start | bytes 100
  17.5 0.9 %copy-start = (s32[1,8,16,128]{3,2,1,0:T(8,128)S(1)}, s32[1,8,16,128]{3,2,1,0:T(8,128)}, u32[]{:S(2)}) copy-start(s32[1,8,16,128]{3,2,1,0:T(8,128)} %param.8) | copy-start | bytes 196612
  20.0 9.2 %collective-permute-start.5 = (f32[8,16,8,128]{3,2,1,0:T(8,128)S(1)}, f32[8,16,8,128]{3,2,1,0:T(8,128)S(1)}, u32[]{:S(2)}, u32[]{:S(2)}) collective-permute-start(f32[8,16,8,128]{3,2,1,0:T(8,128)S(1)} %get-tuple-element.44), channel_id=1, source_target_pairs={{0,64},{64,128},{128,192},{192,0},{1,65},{65,129},{129,193},{193,1... | collective-permute-start | bytes 1572872 | tf_op jit(solution)/shard_map/ppermute | solution.py:241
  20.4 8.8 %collective-permute-start.8 = (f32[8,8,128]{2,1,0:T(8,128)S(1)}, f32[8,8,128]{2,1,0:T(8,128)S(1)}, u32[]{:S(2)}, u32[]{:S(2)}) collective-permute-start(f32[8,8,128]{2,1,0:T(8,128)S(1)} %get-tuple-element.47), channel_id=1, source_target_pairs={{0,7},{1,2},{2,1},{3,4},{4,3},{5,6},{6,5},{7,0},{8,15},{9,10},{10,... | collective-permute-start | bytes 98312 | tf_op jit(solution)/shard_map/ppermute | solution.py:247
  21.9 7.3 %collective-permute-start.9 = (f32[8,8,128]{2,1,0:T(8,128)S(1)}, f32[8,8,128]{2,1,0:T(8,128)S(1)}, u32[]{:S(2)}, u32[]{:S(2)}) collective-permute-start(f32[8,8,128]{2,1,0:T(8,128)S(1)} %get-tuple-element.48), channel_id=1, source_target_pairs={{0,1},{1,0},{2,3},{3,2},{4,5},{5,4},{6,7},{7,6},{8,9},{9,8},{10,11... | collective-permute-start | bytes 98312 | tf_op jit(solution)/shard_map/ppermute | solution.py:248
  22.2 7.1 %collective-permute-start.6 = (f32[16,8,128]{2,1,0:T(8,128)S(1)}, f32[16,8,128]{2,1,0:T(8,128)S(1)}, u32[]{:S(2)}, u32[]{:S(2)}) collective-permute-start(f32[16,8,128]{2,1,0:T(8,128)S(1)} %get-tuple-element.45), channel_id=1, source_target_pairs={{0,8},{8,0},{16,24},{24,16},{32,40},{40,32},{48,56},{56,48},{1,9},... | collective-permute-start | bytes 196616 | tf_op jit(solution)/shard_map/ppermute | solution.py:245
  22.2 7.1 %collective-permute-start.7 = (f32[16,8,128]{2,1,0:T(8,128)S(1)}, f32[16,8,128]{2,1,0:T(8,128)S(1)}, u32[]{:S(2)}, u32[]{:S(2)}) collective-permute-start(f32[16,8,128]{2,1,0:T(8,128)S(1)} %get-tuple-element.46), channel_id=1, source_target_pairs={{0,56},{8,16},{16,8},{24,32},{32,24},{40,48},{48,40},{56,0},{1,57}... | collective-permute-start | bytes 196616 | tf_op jit(solution)/shard_map/ppermute | solution.py:246

commit v3 on v2

--- a/solution.py
+++ b/solution.py
@@ -80,7 +80,7 @@
             zh_ref[x, y], zl_ref[x, y] = split2(mixed)
 
 
-def both_kernel(nx, ny, v_ref, r_ref, uh_ref, ul_ref, zh_ref, zl_ref, rh_ref, rl_ref):
+def both_kernel(nx, ny, v_ref, r_ref, time_ref, uh_ref, ul_ref, zh_ref, zl_ref, rh_ref, rl_ref):
     pack_kernel(nx, ny, v_ref, uh_ref, ul_ref, zh_ref, zl_ref)
     for x in range(nx):
         for y in range(ny):
@@ -277,6 +277,7 @@
     odd_x, odd_y = lax.axis_index("sx") % 2, lax.axis_index("sy") % 2
     place = jnp.where(which == 0, lax.axis_index("tm"), jnp.where(which == 1, odd_x, odd_y))
     vol = volume.reshape(volume.shape[0] * nodes, nodes)
+    small = (vol, face_gain, time_gain.reshape(1, -1))
 
     v, *sent = call(
         functools.partial(prep_kernel, nx, ny), [VMEM, HBM], [field, half] + faces, "prep", stream, grant=52
@@ -284,10 +285,10 @@
     got = exchange(*sent)
     (w,) = call(
         table_kernel, [VMEM] * 4, [shape((8 * nodes, 256), BF16)], "tables", [pltpu.VMEM((128, 128), F32)]
-    )(place, vol, face_gain, time_gain.reshape(1, -1))
+    )(place, *small)
     *views, rh, rl = call(
-        functools.partial(both_kernel, nx, ny), [VMEM] * 2, [packed] * 6, "both"
-    )(v, r)
+        functools.partial(both_kernel, nx, ny), [VMEM] * 3, [packed] * 6, "both"
+    )(v, r, small[2])
     pack = call(functools.partial(pack_kernel, nx, ny), [VMEM], [packed] * 4, "pack")
     scratch = [pltpu.VMEM((n, 16, nz), BF16) for n in (ny, ny, ny, ny, nx, nx, nx, nx)]
     v, *sent = call(

time: 32 us -> 32.3 us (level)
  starting transfers between devices: 19.9 us -> 19.5 us
  waiting for transfers between devices: 2.63 us -> 3.02 us
  local copies, waits for them, and re-layouts: 0.65 us -> 1.04 us
    unnamed x10, local copies, waits for them, and re-layouts: 0.65 us -> 1.04 us
    ppermute x2, starting transfers between devices: 8.49 us -> 8.1 us  [exchange(): lax.ppermute(xb, 'sx', x_two)]
    ppermute x2, waiting for transfers between devices: 2.61 us -> 3 us  [exchange(): lax.ppermute(yb, 'sy', y_two)]
where the time goes in v3:
time: 32.3 us; the launch traced here: 32.2 us
  starting transfers between devices  19.5 us (60%)
  Pallas kernels  8.46 us (26%)
  waiting for transfers between devices  3.02 us (9%)
  local copies, waits for them, and re-layouts  1.04 us (3%)
    ppermute x2, starting transfers between devices, exchange(): lax.ppermute(xb, 'sx', x_two)  8.1 us
    ppermute x2, starting transfers between devices, exchange(): lax.ppermute(yb, 'sy', y_two)  6.42 us
    ppermute x2, starting transfers between devices, exchange(): before = lax.ppermute(up, 'tm', ring('tm', 1))  3.09 us
    ppermute x2, waiting for transfers between devices, exchange(): lax.ppermute(yb, 'sy', y_two)  3 us
    pallas_call x1, Pallas kernels, on_device(): call(functools.partial(sweep_kernel, nx, ny, True), [VMEM] * 15, [shape(c...  2.65 us
    pallas_call x1, Pallas kernels, on_device(): call(functools.partial(prep_kernel, nx, ny), [VMEM, HBM], [field, half] +...  1.68 us
    ppermute x2, starting transfers between devices, exchange(): lax.ppermute(xa, 'sx', x_one)  1.64 us
    pallas_call x1, Pallas kernels, on_device(): call(functools.partial(sweep_kernel, nx, ny, False), [VMEM] * 15, [field,...  1.53 us
  transfers between devices with their start and end apart: 10, of which 1 were waited for; matrix products, arithmetic and copies ran while one was open for 0% of the time, Pallas kernels for 8%

profile of v3, /device:TPU:1, one launch (start us, length us, event | category | flops | bytes accessed | tf_op | source)
XLA Modules:
  0.0 32.2 jit_solution(12996319288223092738)
XLA Ops:
  0.0 0.1 broadcast_select_fusion.place_ref.refs_0_
  0.1 1.7 %prep.1 = (f32[8,16,16,128]{3,2,1,0:T(8,128)S(1)}, f32[8,16,8,128]{3,2,1,0:T(8,128)S(1)}, f32[16,8,128]{2,1,0:T(8,128)S(1)}, f32[16,8,128]{2,1,0:T(8,128)S(1)}, ...) custom-call(s32[3,8,128]{2,1,0:T(8,128)S(1)} %broadcast_select_fusion.place_ref.refs_0_, f32[16,128,128]{2,1,0:T(8,128)} %bitcast.12), custom_call_target="tpu_custom_call" | custom-call | flops 1000000000 | bytes 4000000 | tf_op jit(solution)/shard_map/prep/pallas_call | solution.py:282
  1.8 2.7 %collective-permute-start = (f32[8,16,8,128]{3,2,1,0:T(8,128)S(1)}, f32[8,16,8,128]{3,2,1,0:T(8,128)S(1)}, u32[]{:S(2)}, u32[]{:S(2)}) collective-permute-start(f32[8,16,8,128]{3,2,1,0:T(8,128)S(1)} %get-tuple-element.34), channel_id=1, source_target_pairs={{0,64},{64,128},{128,192},{192,0},{1,65},{65,129},{129,193},{193,1... | collective-permute-start | bytes 1572872 | tf_op jit(solution)/shard_map/ppermute | solution.py:241
  4.5 4.9 %collective-permute-start.3 = (f32[8,8,128]{2,1,0:T(8,128)S(1)}, f32[8,8,128]{2,1,0:T(8,128)S(1)}, u32[]{:S(2)}, u32[]{:S(2)}) collective-permute-start(f32[8,8,128]{2,1,0:T(8,128)S(1)} %get-tuple-element.37), channel_id=1, source_target_pairs={{0,7},{1,2},{2,1},{3,4},{4,3},{5,6},{6,5},{7,0},{8,15},{9,10},{10,... | collective-permute-start | bytes 98312 | tf_op jit(solution)/shard_map/ppermute | solution.py:247
  9.4 0.0 collective-permute-start.4
  9.4 1.6 %collective-permute-start.1 = (f32[16,8,128]{2,1,0:T(8,128)S(1)}, f32[16,8,128]{2,1,0:T(8,128)S(1)}, u32[]{:S(2)}, u32[]{:S(2)}) collective-permute-start(f32[16,8,128]{2,1,0:T(8,128)S(1)} %get-tuple-element.35), channel_id=1, source_target_pairs={{0,8},{8,0},{16,24},{24,16},{32,40},{40,32},{48,56},{56,48},{1,9},... | collective-permute-start | bytes 196616 | tf_op jit(solution)/shard_map/ppermute | solution.py:245
  11.0 4.7 %collective-permute-start.2 = (f32[16,8,128]{2,1,0:T(8,128)S(1)}, f32[16,8,128]{2,1,0:T(8,128)S(1)}, u32[]{:S(2)}, u32[]{:S(2)}) collective-permute-start(f32[16,8,128]{2,1,0:T(8,128)S(1)} %get-tuple-element.36), channel_id=1, source_target_pairs={{0,56},{8,16},{16,8},{24,32},{32,24},{40,48},{48,40},{56,0},{1,57}... | collective-permute-start | bytes 196616 | tf_op jit(solution)/shard_map/ppermute | solution.py:246
  15.7 0.0 copy-done.2
  15.7 0.0 copy-done.3
  15.7 0.6 %copy-done.4 = f32[8]{0:T(128)S(1)} copy-done((f32[8]{0:T(128)S(1)}, f32[8]{0:T(128)}, u32[]{:S(2)}) %copy-start.4) | copy-done | bytes 56
  16.3 0.8 %tables.1.refs_1_ = bf16[128,256]{1,0:T(8,128)(2,1)S(1)} custom-call(s32[3,8,128]{2,1,0:T(8,128)S(1)} %broadcast_select_fusion.place_ref.refs_0_, f32[128,16]{1,0:T(8,128)S(1)} %bitcast.9, f32[8,6]{1,0:T(8,128)S(1)} %copy-done.3, f32[1,8]{1,0:T(1,128)S(1)} %bitcast.10), custom_call_target="tpu_custom_call" | custom-call | flops 1000000000 | bytes 4000000 | tf_op jit(solution)/shard_map/tables/pallas_call | solution.py:286
  17.2 0.4 %copy-done.1 = f32[1,16,8,16,128]{4,3,2,1,0:T(8,128)S(1)} copy-done((f32[1,16,8,16,128]{4,3,2,1,0:T(8,128)S(1)}, f32[1,16,8,16,128]{4,3,2,1,0:T(8,128)}, u32[]{:S(2)}) %copy-start.1) | copy-done | bytes 1048600
  17.5 1.1 %both.1 = (bf16[8,16,16,128]{3,2,1,0:T(8,128)(2,1)S(1)}, bf16[8,16,16,128]{3,2,1,0:T(8,128)(2,1)S(1)}, bf16[8,16,16,128]{3,2,1,0:T(8,128)(2,1)S(1)}, bf16[8,16,1...) custom-call(f32[8,16,16,128]{3,2,1,0:T(8,128)S(1)} %get-tuple-element.27.v_ref., ...), custom_call_target="tpu_custom_call" | custom-call | flops 1000000000 | bytes 4000000 | tf_op jit(solution)/shard_map/both/pallas_call | solution.py:289
  18.7 0.0 collective-permute-done.3.refs_13_
  18.7 0.0 collective-permute-done.4.refs_14_
  18.7 0.0 collective-permute-done.1.refs_11_
  18.7 0.0 collective-permute-done.2.refs_12_
  18.7 0.0 collective-permute-done.refs_10_
  18.7 0.0 copy-done
  18.8 1.5 %sweep_a.1 = (f32[8,16,16,128]{3,2,1,0:T(8,128)S(1)}, f32[8,16,8,128]{3,2,1,0:T(8,128)S(1)}, f32[16,8,128]{2,1,0:T(8,128)S(1)}, f32[16,8,128]{2,1,0:T(8,128)S(1)...) custom-call(s32[3,8,128]{2,1,0:T(8,128)S(1)} %broadcast_select_fusion.place_ref.refs_0_, ...), custom_call_target="tpu_custom_call" | custom-call | flops 1000000000 | bytes 4000000 | tf_op jit(solution)/shard_map/sweep_a/pallas_call | solution.py:294
  20.3 0.4 %collective-permute-start.5 = (f32[8,16,8,128]{3,2,1,0:T(8,128)S(1)}, f32[8,16,8,128]{3,2,1,0:T(8,128)S(1)}, u32[]{:S(2)}, u32[]{:S(2)}) collective-permute-start(f32[8,16,8,128]{3,2,1,0:T(8,128)S(1)} %get-tuple-element.44), channel_id=1, source_target_pairs={{0,64},{64,128},{128,192},{192,0},{1,65},{65,129},{129,193},{193,1... | collective-permute-start | bytes 1572872 | tf_op jit(solution)/shard_map/ppermute | solution.py:241
  20.7 1.5 %collective-permute-start.8 = (f32[8,8,128]{2,1,0:T(8,128)S(1)}, f32[8,8,128]{2,1,0:T(8,128)S(1)}, u32[]{:S(2)}, u32[]{:S(2)}) collective-permute-start(f32[8,8,128]{2,1,0:T(8,128)S(1)} %get-tuple-element.47), channel_id=1, source_target_pairs={{0,7},{1,2},{2,1},{3,4},{4,3},{5,6},{6,5},{7,0},{8,15},{9,10},{10,... | collective-permute-start | bytes 98312 | tf_op jit(solution)/shard_map/ppermute | solution.py:247
  22.2 0.2 collective-permute-start.9
  22.4 0.0 collective-permute-start.6
  22.4 3.4 %collective-permute-start.7 = (f32[16,8,128]{2,1,0:T(8,128)S(1)}, f32[16,8,128]{2,1,0:T(8,128)S(1)}, u32[]{:S(2)}, u32[]{:S(2)}) collective-permute-start(f32[16,8,128]{2,1,0:T(8,128)S(1)} %get-tuple-element.46), channel_id=1, source_target_pairs={{0,56},{8,16},{16,8},{24,32},{32,24},{40,48},{48,40},{56,0},{1,57}... | collective-permute-start | bytes 196616 | tf_op jit(solution)/shard_map/ppermute | solution.py:246
  25.9 0.6 %pack.1 = (bf16[8,16,16,128]{3,2,1,0:T(8,128)(2,1)S(1)}, bf16[8,16,16,128]{3,2,1,0:T(8,128)(2,1)S(1)}, bf16[8,16,16,128]{3,2,1,0:T(8,128)(2,1)S(1)}, bf16[8,16,16,128]{3,2,1,0:T(8,128)(2,1)S(1)}) custom-call(f32[8,16,16,128]{3,2,1,0:T(8,128)S(1)} %get-tuple-element.39.v_ref.refs_3_), custom_call_target="tpu_custom_call" | custom-call | flops 1000000000 | bytes 4000000 | tf_op jit(solution)/shard_map/pack/pallas_call | solution.py:299
  26.5 3.0 %collective-permute-done.8.refs_13_ = f32[8,8,128]{2,1,0:T(8,128)S(1)} collective-permute-done((f32[8,8,128]{2,1,0:T(8,128)S(1)}, f32[8,8,128]{2,1,0:T(8,128)S(1)}, u32[]{:S(2)}, u32[]{:S(2)}) %collective-permute-start.8) | collective-permute-done | bytes 32800 | tf_op jit(solution)/shard_map/ppermute | solution.py:247
  29.5 0.0 collective-permute-done.9.refs_14_
  29.5 0.0 collective-permute-done.6.refs_11_
  29.5 0.0 collective-permute-done.7.refs_12_
  29.5 0.0 collective-permute-done.5.refs_10_
  29.5 2.7 %sweep_b.1 = f32[16,128,128]{2,1,0:T(8,128)} custom-call(s32[3,8,128]{2,1,0:T(8,128)S(1)} %broadcast_select_fusion.place_ref.refs_0_, bf16[128,256]{1,0:T(8,128)(2,1)S(1)} %tables.1.refs_1_, s32[8,16,128]{2,1,0:T(8,128)S(1)} %bitcast.7, f32[8,16,16,128]{3,2,1,0:T(8,128)S(1)} %get-tuple-element.39.v_ref.refs_3_, ...), custom_call_target="tpu_custom_call" | custom-call | flops 1000000000 | bytes 4000000 | tf_op jit(solution)/shard_map/sweep_b/pallas_call | solution.py:300
  (7 shorter events, 0.0 us)
Async XLA Ops:
  0.1 15.6 %copy-start.2 = (f32[8,16,16]{2,1,0:T(8,128)S(1)}, f32[8,16,16]{2,1,0:T(8,128)}, u32[]{:S(2)}) copy-start(f32[8,16,16]{2,1,0:T(8,128)} %param.9) | copy-start | bytes 24580
  1.8 17.0 %collective-permute-start = (f32[8,16,8,128]{3,2,1,0:T(8,128)S(1)}, f32[8,16,8,128]{3,2,1,0:T(8,128)S(1)}, u32[]{:S(2)}, u32[]{:S(2)}) collective-permute-start(f32[8,16,8,128]{3,2,1,0:T(8,128)S(1)} %get-tuple-element.34), channel_id=1, source_target_pairs={{0,64},{64,128},{128,192},{192,0},{1,65},{65,129},{129,193},{193,1... | collective-permute-start | bytes 1572872 | tf_op jit(solution)/shard_map/ppermute | solution.py:241
  4.5 14.2 %collective-permute-start.3 = (f32[8,8,128]{2,1,0:T(8,128)S(1)}, f32[8,8,128]{2,1,0:T(8,128)S(1)}, u32[]{:S(2)}, u32[]{:S(2)}) collective-permute-start(f32[8,8,128]{2,1,0:T(8,128)S(1)} %get-tuple-element.37), channel_id=1, source_target_pairs={{0,7},{1,2},{2,1},{3,4},{4,3},{5,6},{6,5},{7,0},{8,15},{9,10},{10,... | collective-permute-start | bytes 98312 | tf_op jit(solution)/shard_map/ppermute | solution.py:247
  9.4 6.3 %copy-start.3 = (f32[8,6]{1,0:T(8,128)S(1)}, f32[8,6]{1,0:T(8,128)}, u32[]{:S(2)}) copy-start(f32[8,6]{1,0:T(8,128)} %face_ref.1) | copy-start | bytes 580
  9.4 9.3 %collective-permute-start.4 = (f32[8,8,128]{2,1,0:T(8,128)S(1)}, f32[8,8,128]{2,1,0:T(8,128)S(1)}, u32[]{:S(2)}, u32[]{:S(2)}) collective-permute-start(f32[8,8,128]{2,1,0:T(8,128)S(1)} %get-tuple-element.38), channel_id=1, source_target_pairs={{0,1},{1,0},{2,3},{3,2},{4,5},{5,4},{6,7},{7,6},{8,9},{9,8},{10,11... | collective-permute-start | bytes 98312 | tf_op jit(solution)/shard_map/ppermute | solution.py:248
  9.4 9.4 %collective-permute-start.1 = (f32[16,8,128]{2,1,0:T(8,128)S(1)}, f32[16,8,128]{2,1,0:T(8,128)S(1)}, u32[]{:S(2)}, u32[]{:S(2)}) collective-permute-start(f32[16,8,128]{2,1,0:T(8,128)S(1)} %get-tuple-element.35), channel_id=1, source_target_pairs={{0,8},{8,0},{16,24},{24,16},{32,40},{40,32},{48,56},{56,48},{1,9},... | collective-permute-start | bytes 196616 | tf_op jit(solution)/shard_map/ppermute | solution.py:245
  11.0 7.7 %collective-permute-start.2 = (f32[16,8,128]{2,1,0:T(8,128)S(1)}, f32[16,8,128]{2,1,0:T(8,128)S(1)}, u32[]{:S(2)}, u32[]{:S(2)}) collective-permute-start(f32[16,8,128]{2,1,0:T(8,128)S(1)} %get-tuple-element.36), channel_id=1, source_target_pairs={{0,56},{8,16},{16,8},{24,32},{32,24},{40,48},{48,40},{56,0},{1,57}... | collective-permute-start | bytes 196616 | tf_op jit(solution)/shard_map/ppermute | solution.py:246
  15.7 0.7 %copy-start.4 = (f32[8]{0:T(128)S(1)}, f32[8]{0:T(128)}, u32[]{:S(2)}) copy-start(f32[8]{0:T(128)} %param.11) | copy-start | bytes 100
  16.3 1.2 %copy-start.1 = (f32[1,16,8,16,128]{4,3,2,1,0:T(8,128)S(1)}, f32[1,16,8,16,128]{4,3,2,1,0:T(8,128)}, u32[]{:S(2)}) copy-start(f32[1,16,8,16,128]{4,3,2,1,0:T(8,128)} %param.6) | copy-start | bytes 3145732
  17.5 1.2 %copy-start = (s32[1,8,16,128]{3,2,1,0:T(8,128)S(1)}, s32[1,8,16,128]{3,2,1,0:T(8,128)}, u32[]{:S(2)}) copy-start(s32[1,8,16,128]{3,2,1,0:T(8,128)} %param.8) | copy-start | bytes 196612
  20.3 9.2 %collective-permute-start.5 = (f32[8,16,8,128]{3,2,1,0:T(8,128)S(1)}, f32[8,16,8,128]{3,2,1,0:T(8,128)S(1)}, u32[]{:S(2)}, u32[]{:S(2)}) collective-permute-start(f32[8,16,8,128]{3,2,1,0:T(8,128)S(1)} %get-tuple-element.44), channel_id=1, source_target_pairs={{0,64},{64,128},{128,192},{192,0},{1,65},{65,129},{129,193},{193,1... | collective-permute-start | bytes 1572872 | tf_op jit(solution)/shard_map/ppermute | solution.py:241
  20.7 8.8 %collective-permute-start.8 = (f32[8,8,128]{2,1,0:T(8,128)S(1)}, f32[8,8,128]{2,1,0:T(8,128)S(1)}, u32[]{:S(2)}, u32[]{:S(2)}) collective-permute-start(f32[8,8,128]{2,1,0:T(8,128)S(1)} %get-tuple-element.47), channel_id=1, source_target_pairs={{0,7},{1,2},{2,1},{3,4},{4,3},{5,6},{6,5},{7,0},{8,15},{9,10},{10,... | collective-permute-start | bytes 98312 | tf_op jit(solution)/shard_map/ppermute | solution.py:247
  22.2 7.3 %collective-permute-start.9 = (f32[8,8,128]{2,1,0:T(8,128)S(1)}, f32[8,8,128]{2,1,0:T(8,128)S(1)}, u32[]{:S(2)}, u32[]{:S(2)}) collective-permute-start(f32[8,8,128]{2,1,0:T(8,128)S(1)} %get-tuple-element.48), channel_id=1, source_target_pairs={{0,1},{1,0},{2,3},{3,2},{4,5},{5,4},{6,7},{7,6},{8,9},{9,8},{10,11... | collective-permute-start | bytes 98312 | tf_op jit(solution)/shard_map/ppermute | solution.py:248
  22.4 7.0 %collective-permute-start.6 = (f32[16,8,128]{2,1,0:T(8,128)S(1)}, f32[16,8,128]{2,1,0:T(8,128)S(1)}, u32[]{:S(2)}, u32[]{:S(2)}) collective-permute-start(f32[16,8,128]{2,1,0:T(8,128)S(1)} %get-tuple-element.45), channel_id=1, source_target_pairs={{0,8},{8,0},{16,24},{24,16},{32,40},{40,32},{48,56},{56,48},{1,9},... | collective-permute-start | bytes 196616 | tf_op jit(solution)/shard_map/ppermute | solution.py:245
  22.4 7.0 %collective-permute-start.7 = (f32[16,8,128]{2,1,0:T(8,128)S(1)}, f32[16,8,128]{2,1,0:T(8,128)S(1)}, u32[]{:S(2)}, u32[]{:S(2)}) collective-permute-start(f32[16,8,128]{2,1,0:T(8,128)S(1)} %get-tuple-element.46), channel_id=1, source_target_pairs={{0,56},{8,16},{16,8},{24,32},{32,24},{40,48},{48,40},{56,0},{1,57}... | collective-permute-start | bytes 196616 | tf_op jit(solution)/shard_map/ppermute | solution.py:246
